TPU v7x, 32 devices: a whole 2x2x4 slice. The times are simulated.
32 devices in a mesh: dp: 8 (over y, x, core), mp: 4 (over z).
Axes of the slice: x: 2, y: 2, z: 4, core: 2. Of those that a mesh axis runs over, the one named last changes fastest.
Arguments:
- query_hidden: bfloat16 [4096, 4096], P('dp'), may hold values from -6 to 6
- passage_hidden: bfloat16 [4096, 4096], P('dp'), may hold values from -6 to 6
- head_weight: bfloat16 [4096, 4096], P(None, 'mp'), may hold values from -0.09375 to 0.09375
- neg_blocks: int32 [32, 4], P('dp'), may hold values from 0 to 31, as said below
- pos_ids: int32 [4096], P('dp'), may hold values from 0 to 127
Outputs:
- query_loss: float32 [4096], P('dp')
- grad_weight: float32 [4096, 4096], P('dp', 'mp')
- grad_query_hidden: bfloat16 [4096, 4096], P('dp', 'mp')
- grad_passage_hidden: bfloat16 [4096, 4096], P('dp', 'mp')
Inputs may be any that keep to these rules, and one draw needn't show every extreme that they name: `neg_blocks`: within each aligned group of 4 query blocks all 16 ids are different, and at most 2 of them fall into any one aligned group of 4 passage block ids; some group of passage blocks receives exactly 2 of them.
All inputs are finite; a program needn't handle non-finite values.
Results may differ from a plain program's by a relative error of at most 0.017.
Values may be sent and summed in bfloat16 or wider, within the bound.
No kernel may reach another device: no remote copies, remote signals or barrier semaphores. Data moves between devices by JAX's collectives and lax.ppermute only.
A program may use at most 128 MiB of HBM per device.

v0:
```python
import jax
import jax.numpy as jnp
from jax import lax
from jax.sharding import PartitionSpec as P

logit_divisor = 0.02
epsilon = 1e-06


def back_norm(inverse, unit_rows, d_unit, inner):
    return (inverse[:, None] * (d_unit - unit_rows * inner[:, None])).astype(jnp.bfloat16)


def local(query_hidden, passage_hidden, head_weight, neg_blocks, pos_ids):
    dp_count = lax.axis_size("dp")
    block_count, neg_count = neg_blocks.shape
    row_count = query_hidden.shape[0]
    block_rows = row_count // block_count
    embed_width = head_weight.shape[1]
    cand_rows = (1 + neg_count) * block_rows
    request_count = block_count * neg_count
    slot_depth = (request_count + dp_count - 1) // dp_count
    slot_count = dp_count * slot_depth
    query_embed = jnp.dot(query_hidden, head_weight, preferred_element_type=jnp.float32)
    passage_embed = jnp.dot(passage_hidden, head_weight, preferred_element_type=jnp.float32)
    query_sq, passage_sq = lax.psum(
        (
            jnp.sum(query_embed * query_embed, axis=1),
            jnp.sum(passage_embed * passage_embed, axis=1),
        ),
        "mp",
    )
    query_inv = lax.rsqrt(query_sq + epsilon)
    passage_inv = lax.rsqrt(passage_sq + epsilon)
    query_unit = query_embed * query_inv[:, None]
    passage_unit = passage_embed * passage_inv[:, None]
    query_norm = query_unit.astype(jnp.bfloat16)
    passage_norm = passage_unit.astype(jnp.bfloat16)
    query_blocks = query_norm.reshape(block_count, block_rows, embed_width)
    passage_blocks = passage_norm.reshape(block_count, block_rows, embed_width)
    wanted = neg_blocks.reshape(-1)
    owners = wanted // block_count
    local_ids = wanted % block_count
    request_order = jnp.arange(request_count, dtype=jnp.int32)
    earlier_same = (owners[:, None] == owners[None, :]) & (
        request_order[None, :] < request_order[:, None]
    )
    owner_rank = jnp.sum(earlier_same.astype(jnp.int32), axis=1)
    slot_of = owners * slot_depth + owner_rank
    slot_table = (slot_of[:, None] == jnp.arange(slot_count, dtype=jnp.int32)[None, :]).astype(
        jnp.int32
    )
    requests = jnp.sum(slot_table * (local_ids + 1)[:, None], axis=0).reshape(dp_count, slot_depth)
    asked = lax.all_to_all(requests, "dp", split_axis=0, concat_axis=0, tiled=True).reshape(
        slot_count
    )
    live_slots = (asked > 0).astype(jnp.bfloat16)
    picked = jnp.take(passage_blocks, jnp.maximum(asked - 1, 0), axis=0) * live_slots[:, None, None]
    reply = picked.reshape(dp_count, slot_depth, block_rows, embed_width)
    arrived = lax.all_to_all(reply, "dp", split_axis=0, concat_axis=0, tiled=True).reshape(
        slot_count, block_rows, embed_width
    )
    fetched = jnp.take(arrived, slot_of, axis=0).reshape(
        block_count, neg_count, block_rows, embed_width
    )
    retrieved_documents = jnp.concatenate([passage_blocks[:, None], fetched], axis=1).reshape(
        block_count, cand_rows, embed_width
    )
    similarity_parts = jnp.einsum(
        "bqe,bce->bqc", query_blocks, retrieved_documents, preferred_element_type=jnp.float32
    )
    positions = pos_ids.reshape(block_count, block_rows)
    similarity_table = (
        lax.psum(similarity_parts.astype(jnp.bfloat16), "mp").astype(jnp.float32) / logit_divisor
    )
    columns = jnp.arange(cand_rows, dtype=jnp.int32)
    matching_document_slot = (columns[None, None, :] == positions[:, :, None]).astype(jnp.float32)
    exponent_values = jnp.exp(similarity_table)
    normalizer_totals = jnp.sum(exponent_values, axis=2)
    losses = jnp.log(normalizer_totals) - jnp.sum(similarity_table * matching_document_slot, axis=2)
    attention_probabilities = (
        (exponent_values / normalizer_totals[:, :, None] - matching_document_slot) / logit_divisor
    ).astype(jnp.bfloat16)
    d_query = jnp.einsum(
        "bqc,bce->bqe",
        attention_probabilities,
        retrieved_documents,
        preferred_element_type=jnp.float32,
    ).reshape(row_count, embed_width)
    d_cand = jnp.einsum(
        "bqc,bqe->bce", attention_probabilities, query_blocks, preferred_element_type=jnp.float32
    )
    own_terms = d_cand[:, :block_rows]
    neg_terms = (
        d_cand[:, block_rows:].reshape(request_count, block_rows, embed_width).astype(jnp.bfloat16)
    )
    outgoing = (
        jnp.zeros((slot_count, block_rows, embed_width), jnp.bfloat16).at[slot_of].set(neg_terms)
    )
    outgoing = outgoing.reshape(dp_count, slot_depth, block_rows, embed_width)
    returned = lax.all_to_all(outgoing, "dp", split_axis=0, concat_axis=0, tiled=True).reshape(
        slot_count, block_rows, embed_width
    )
    selector = (asked[None, :] - 1 == jnp.arange(block_count, dtype=jnp.int32)[:, None]).astype(
        jnp.bfloat16
    )
    d_passage = own_terms + jnp.einsum(
        "ls,sbe->lbe", selector, returned, preferred_element_type=jnp.float32
    )
    d_passage = d_passage.reshape(row_count, embed_width)
    query_inner, passage_inner = lax.psum(
        (jnp.sum(query_unit * d_query, axis=1), jnp.sum(passage_unit * d_passage, axis=1)), "mp"
    )
    d_query_embed = back_norm(query_inv, query_unit, d_query, query_inner)
    d_passage_embed = back_norm(passage_inv, passage_unit, d_passage, passage_inner)
    contract = (((0,), (0,)), ((), ()))
    query_part = lax.dot_general(
        query_hidden, d_query_embed, contract, preferred_element_type=jnp.float32
    )
    passage_part = lax.dot_general(
        passage_hidden, d_passage_embed, contract, preferred_element_type=jnp.float32
    )
    grad_weight = lax.psum_scatter(
        (query_part + passage_part).astype(jnp.bfloat16), "dp", scatter_dimension=0, tiled=True
    ).astype(jnp.float32)
    transpose_dims = (((1,), (1,)), ((), ()))
    query_back = lax.dot_general(
        d_query_embed, head_weight, transpose_dims, preferred_element_type=jnp.float32
    ).astype(jnp.bfloat16)
    passage_back = lax.dot_general(
        d_passage_embed, head_weight, transpose_dims, preferred_element_type=jnp.float32
    ).astype(jnp.bfloat16)
    query_grad, passage_grad = (
        lax.psum_scatter(query_back, "mp", scatter_dimension=1, tiled=True).astype(jnp.float32),
        lax.psum_scatter(passage_back, "mp", scatter_dimension=1, tiled=True).astype(jnp.float32),
    )
    return (
        losses.reshape(row_count),
        grad_weight,
        query_grad.astype(jnp.bfloat16),
        passage_grad.astype(jnp.bfloat16),
    )


def solution(mesh):
    placed = (P("dp", None), P("dp", None), P(None, "mp"), P("dp", None), P("dp"))
    return jax.shard_map(
        local,
        mesh=mesh,
        in_specs=placed,
        out_specs=(P("dp"), P("dp", "mp"), P("dp", "mp"), P("dp", "mp")),
        check_vma=False,
    )
```

profile of v0, /device:TPU:0, one launch (start us, length us, event | category | flops | bytes accessed | tf_op | source)
XLA Modules:
  0.0 533.0 jit_solution(12846390142526082955)
XLA Ops:
  8.9 5.2 all-to-all-start
  14.1 8.4 %multiply_reduce_fusion.1 = (f32[512]{0:T(512)S(1)}, f32[512,1024]{1,0:T(8,128)S(1)}) fusion(bf16[512,4096]{1,0:T(8,128)(2,1)} %param.5, bf16[4096,1024]{1,0:T(8,128)(2,1)} %param.7), kind=kOutput, calls=%fused_computation.23 | convolution fusion | flops 4296015360 | bytes 14682112 | tf_op jit(solution)/shard_map/dot_general | solution.py:24
  22.6 5.8 %multiply_reduce_fusion = (f32[512]{0:T(512)S(1)}, f32[512,1024]{1,0:T(8,128)}) fusion(bf16[512,4096]{1,0:T(8,128)(2,1)S(1)} %copy-done.15, bf16[4096,1024]{1,0:T(8,128)(2,1)S(1)} %copy-done.14), kind=kOutput, calls=%fused_computation.22 | convolution fusion | flops 4296015360 | bytes 14682112 | tf_op jit(solution)/shard_map/dot_general | solution.py:25
  28.4 11.9 %all-reduce.1 = (f32[512]{0:T(512)S(1)}, f32[512]{0:T(512)S(1)}) all-reduce(f32[512]{0:T(512)S(1)} %get-tuple-element.36, f32[512]{0:T(512)S(1)} %get-tuple-element.38), channel_id=1, replica_groups=mesh['dp'=8,'mp'=4] {'mp'}, use_global_device_ids=true, to_apply=%region_3.0 | all-reduce | flops 1024 | bytes 8192 | tf_op jit(solution)/shard_map/psum | solution.py:26
  45.3 4.6 select_multiply_fusion
  49.9 4.7 all-to-all-start.1
  56.2 47.5 %all-to-all-done.1 = bf16[8,2,128,1024]{3,2,1,0:T(8,128)(2,1)} async-done(((bf16[8,2,128,1024]{3,2,1,0:T(8,128)(2,1)}), bf16[8,2,128,1024]{3,2,1,0:T(8,128)(2,1)}, u32[]{:S(2)}, u32[]{:S(2)}) %all-to-all-start.1) | async-done | bytes 4194336 | tf_op jit(solution)/shard_map/all_to_all | solution.py:60
  103.7 5.0 gather_fusion.1
  116.8 37.0 %all-reduce.4.cloned.1.call-done = bf16[4,128,640]{2,1,0:T(8,128)(2,1)} async-done(((bf16[4,128,640]{2,1,0:T(8,128)(2,1)}), bf16[4,128,640]{2,1,0:T(8,128)(2,1)}) %all-reduce.4.cloned.1.call-update) | async-done | bytes 655376 | tf_op jit(solution)/shard_map/psum | solution.py:74
  158.2 4.0 copy-done
  167.3 10.9 %scatter_fusion = bf16[16,128,1024]{2,1,0:T(8,128)(2,1)} fusion(bf16[16,128,1024]{2,1,0:T(8,128)(2,1)} %broadcast_in_dim.26, s32[16]{0:T(128)S(1)} %fusion.20, bf16[16,128,1024]{2,1,0:T(8,128)(2,1)} %bitcast.79), kind=kCustom, calls=%fused_computation.2 | custom fusion | bytes 12582976 | tf_op jit(solution)/shard_map/scatter | solution.py:98
  178.2 8.5 %copy.57 = bf16[8,2,128,1024]{3,1,2,0:T(2,128)(2,1)} copy(bf16[8,2,128,1024]{3,2,1,0:T(8,128)(2,1)} %bitcast.72) | data formatting | bytes 8388608 | tf_op jit(solution)/shard_map/reshape | solution.py:100
  186.6 4.7 all-to-all-start.2
  197.3 43.2 %all-to-all-done.2 = bf16[8,2,128,1024]{3,1,2,0:T(2,128)(2,1)} async-done(((bf16[8,2,128,1024]{3,1,2,0:T(2,128)(2,1)}), bf16[8,2,128,1024]{3,1,2,0:T(2,128)(2,1)}, u32[]{:S(2)}, u32[]{:S(2)}) %all-to-all-start.2) | async-done | bytes 4194336 | tf_op jit(solution)/shard_map/all_to_all | solution.py:101
  240.4 8.9 %copy.58 = bf16[8,2,128,1024]{3,1,0,2:T(2,128)(2,1)} copy(bf16[8,2,128,1024]{3,1,2,0:T(2,128)(2,1)} %all-to-all-done.2) | data formatting | bytes 8388608 | tf_op jit(solution)/shard_map/all_to_all | solution.py:101
  249.3 7.2 %reshape.291 = bf16[16,128,1024]{2,0,1:T(8,128)(2,1)} reshape(bf16[8,2,128,1024]{3,1,0,2:T(2,128)(2,1)} %copy.58) | data formatting | bytes 8388608 | tf_op jit(solution)/shard_map/reshape | solution.py:101
  264.3 10.5 %all-reduce = (f32[512]{0:T(512)S(1)}, f32[512]{0:T(512)S(1)}) all-reduce(f32[512]{0:T(512)S(1)} %fusion.4, f32[512]{0:T(512)S(1)} %fusion.1), channel_id=1, replica_groups=mesh['dp'=8,'mp'=4] {'mp'}, use_global_device_ids=true, to_apply=%region_10.11 | all-reduce | flops 1024 | bytes 8192 | tf_op jit(solution)/shard_map/psum | solution.py:111
  279.3 8.2 %fusion.23 = f32[1024,4096]{1,0:T(8,128)} fusion(bf16[512,1024]{1,0:T(8,128)(2,1)S(1)} %fusion.6, bf16[512,4096]{1,0:T(8,128)(2,1)S(1)} %copy-done.8), kind=kOutput, calls=%fused_computation.79 | convolution fusion | flops 4294967296 | bytes 22020096 | tf_op jit(solution)/shard_map/dot_general | solution.py:117
  287.5 11.4 %fusion = bf16[4096,1024]{0,1:T(8,128)(2,1)} fusion(f32[1024,4096]{1,0:T(8,128)} %fusion.23, bf16[512,1024]{1,0:T(8,128)(2,1)S(1)} %fusion.3, bf16[512,4096]{1,0:T(8,128)(2,1)} %param.6), kind=kOutput, calls=%fused_computation.4 | convolution fusion | flops 4303355904 | bytes 30408704 | tf_op jit(solution)/shard_map/dot_general | solution.py:120
  298.9 10.1 %convolution_convert_fusion.1 = bf16[512,4096]{1,0:T(8,128)(2,1)} fusion(bf16[512,1024]{1,0:T(8,128)(2,1)S(1)} %fusion.6, bf16[4096,1024]{1,0:T(8,128)(2,1)} %param.7), kind=kOutput, calls=%fused_computation.7 | convolution fusion | flops 4297064448 | bytes 13631488 | tf_op jit(solution)/shard_map/dot_general | solution.py:127
  310.5 9.8 %convolution_convert_fusion = bf16[512,4096]{1,0:T(8,128)(2,1)} fusion(bf16[512,1024]{1,0:T(8,128)(2,1)S(1)} %copy-done.11, bf16[4096,1024]{1,0:T(8,128)(2,1)} %param.7), kind=kOutput, calls=%fused_computation.6 | convolution fusion | flops 4297064448 | bytes 13631488 | tf_op jit(solution)/shard_map/dot_general | solution.py:130
  320.9 45.8 %reduce-scatter.4.cloned.1.call-done = bf16[512,1024]{0,1:T(8,128)(2,1)} async-done(((bf16[4096,1024]{0,1:T(8,128)(2,1)}), bf16[512,1024]{0,1:T(8,128)(2,1)}) %reduce-scatter.4.cloned.1.call-update) | async-done | bytes 1048592 | tf_op jit(solution)/shard_map/reduce_scatter | solution.py:123
  369.3 77.2 %reduce-scatter.6.cloned.1.call-done = bf16[512,1024]{1,0:T(8,128)(2,1)} async-done(((bf16[512,4096]{1,0:T(8,128)(2,1)}), bf16[512,1024]{1,0:T(8,128)(2,1)}) %reduce-scatter.6.cloned.1.call-update) | async-done | bytes 1048592 | tf_op jit(solution)/shard_map/reduce_scatter | solution.py:134
  446.5 80.0 %reduce-scatter.8.cloned.1.call-done = bf16[512,1024]{1,0:T(8,128)(2,1)} async-done(((bf16[512,4096]{1,0:T(8,128)(2,1)}), bf16[512,1024]{1,0:T(8,128)(2,1)}) %reduce-scatter.8.cloned.1.call-update) | async-done | bytes 1048592 | tf_op jit(solution)/shard_map/reduce_scatter | solution.py:135
  (81 shorter events, 48.5 us)
Async XLA Ops:
  8.9 33.2 %all-to-all-start = ((s32[8,1,2]{2,1,0:T(1,128)}), s32[8,1,2]{2,1,0:T(1,128)S(1)}, u32[]{:S(2)}, u32[]{:S(2)}) async-start(s32[8,1,2]{2,1,0:T(1,128)} %bitcast.3), calls=%async_computation | async-start | bytes 8192 | tf_op jit(solution)/shard_map/all_to_all | solution.py:54
  14.1 8.5 %copy-start.14 = (bf16[4096,1024]{1,0:T(8,128)(2,1)S(1)}, bf16[4096,1024]{1,0:T(8,128)(2,1)}, u32[]{:S(2)}) copy-start(bf16[4096,1024]{1,0:T(8,128)(2,1)} %param.7) | copy-start | bytes 25165828
  14.1 8.5 %copy-start.15 = (bf16[512,4096]{1,0:T(8,128)(2,1)S(1)}, bf16[512,4096]{1,0:T(8,128)(2,1)}, u32[]{:S(2)}) copy-start(bf16[512,4096]{1,0:T(8,128)(2,1)} %param.6) | copy-start | bytes 12582916
  49.9 4.9 copy-start.13
  49.9 53.8 %all-to-all-start.1 = ((bf16[8,2,128,1024]{3,2,1,0:T(8,128)(2,1)}), bf16[8,2,128,1024]{3,2,1,0:T(8,128)(2,1)}, u32[]{:S(2)}, u32[]{:S(2)}) async-start(bf16[8,2,128,1024]{3,2,1,0:T(8,128)(2,1)} %select_multiply_fusion), calls=%async_computation.1 | async-start | bytes 8388608 | tf_op jit(solution)/shard_map/all_to_all | solution.py:60
  54.6 99.2 %all-reduce.4.cloned.1.call-start = ((), (), s32[]{:S(2)}) async-start(), calls=%async_computation.6 | async-start | bytes 1310720 | tf_op jit(solution)/shard_map/psum | solution.py:74
  111.3 2.8 copy-start.4
  111.8 2.4 copy-start.1
  111.8 42.0 %copy-start.12 = (s32[512]{0:T(512)S(1)}, s32[512]{0:T(512)}, u32[]{:S(2)}) copy-start(s32[512]{0:T(512)} %param.9) | copy-start | bytes 6148
  111.8 43.6 %copy-start.5 = (bf16[512,1024]{1,0:T(8,128)(2,1)S(1)}, bf16[512,1024]{1,0:T(8,128)(2,1)}, u32[]{:S(2)}) copy-start(bf16[512,1024]{1,0:T(8,128)(2,1)} %multiply_convert_fusion.1) | copy-start | bytes 3145732
  158.2 4.0 copy-start
  186.6 5.1 copy-start.9
  186.6 53.8 %all-to-all-start.2 = ((bf16[8,2,128,1024]{3,1,2,0:T(2,128)(2,1)}), bf16[8,2,128,1024]{3,1,2,0:T(2,128)(2,1)}, u32[]{:S(2)}, u32[]{:S(2)}) async-start(bf16[8,2,128,1024]{3,1,2,0:T(2,128)(2,1)} %copy.57), calls=%async_computation.2 | async-start | bytes 8388608 | tf_op jit(solution)/shard_map/all_to_all | solution.py:101
  191.3 175.4 %reduce-scatter.4.cloned.1.call-start = ((), (), s32[]{:S(2)}) async-start(), calls=%async_computation.7 | async-start | bytes 9437184 | tf_op jit(solution)/shard_map/reduce_scatter | solution.py:123
  195.5 1.3 copy-start.6
  259.5 4.4 copy-start.2
  262.5 1.4 copy-start.3
  274.8 2.9 copy-start.7
  274.8 4.5 copy-start.8
  277.6 9.9 %copy-start.10 = (bf16[512,1024]{1,0:T(8,128)(2,1)}, bf16[512,1024]{1,0:T(8,128)(2,1)S(1)}, u32[]{:S(2)}) copy-start(bf16[512,1024]{1,0:T(8,128)(2,1)S(1)} %fusion.3) | copy-start | bytes 3145732
  298.9 147.6 %reduce-scatter.6.cloned.1.call-start = ((), (), s32[]{:S(2)}) async-start(), calls=%async_computation.8 | async-start | bytes 5242880 | tf_op jit(solution)/shard_map/reduce_scatter | solution.py:134
  309.1 1.5 copy-start.11
  309.1 217.4 %reduce-scatter.8.cloned.1.call-start = ((), (), s32[]{:S(2)}) async-start(), calls=%async_computation.9 | async-start | bytes 5242880 | tf_op jit(solution)/shard_map/reduce_scatter | solution.py:135
Sparse Core Ops, SparseCore 0:
  116.9 36.8 all-reduce.3
  299.0 67.6 reduce-scatter.3
  369.7 76.7 reduce-scatter.5
  449.2 77.2 reduce-scatter.7
where the time goes:
time: 534 us; the launch traced here: 533 us
  waiting for transfers between devices  331 us (62%)
  matrix products  65.8 us (12%)
  local copies, waits for them, and re-layouts  64.7 us (12%)
  blocking collectives  22.5 us (4%)
  other arithmetic  20.2 us (4%)
  starting transfers between devices  15.1 us (3%)
  between operations  14 us (3%)
    reduce_scatter x1, waiting for transfers between devices, local(): lax.psum_scatter(passage_back, 'mp', scatter_dimension=1, tiled=True)  80 us
    reduce_scatter x1, waiting for transfers between devices, local(): lax.psum_scatter(query_back, 'mp', scatter_dimension=1, tiled=True)  77.2 us
    all_to_all x1, waiting for transfers between devices, local(): lax.all_to_all(reply, 'dp', split_axis=0, concat_axis=0, tiled=True)  47.5 us
    reduce_scatter x1, waiting for transfers between devices, local(): lax.psum_scatter((query_part + passage_part).astype(jnp.bfloat16), 'dp',...  45.8 us
    all_to_all x1, waiting for transfers between devices, local(): lax.all_to_all(outgoing, 'dp', split_axis=0, concat_axis=0, tiled=True)  43.2 us
    psum x1, waiting for transfers between devices, local(): lax.psum(similarity_parts.astype(jnp.bfloat16), 'mp').astype(jnp.float32)  37 us
    unnamed x33, local copies, waits for them, and re-layouts  14.2 us
    psum x1, blocking collectives, local(): lax.psum((jnp.sum(query_embed * query_embed, axis=1), jnp.sum(passage_emb...  11.9 us
  transfers between devices with their start and end apart: 7, of which 6 were waited for; matrix products, arithmetic and copies ran while one was open for 8% of the time, Pallas kernels for 0%

commit v1 on v0

--- a/solution.py
+++ b/solution.py
@@ -1,17 +1,789 @@
+import functools
+
 import jax
 import jax.numpy as jnp
 from jax import lax
+from jax.experimental import pallas as pl
+from jax.experimental.pallas import tpu as pltpu
 from jax.sharding import PartitionSpec as P
 
 logit_divisor = 0.02
 epsilon = 1e-06
+f32 = jnp.float32
+bf16 = jnp.bfloat16
+MIB = 1024 * 1024
+EXT = 16
+NT = (((1,), (1,)), ((), ()))
+NN = (((1,), (0,)), ((), ()))
+TN = (((0,), (0,)), ((), ()))
+
+
+def mm(a, b, dims):
+    return lax.dot_general(a, b, dims, preferred_element_type=f32)
+
+
+def as_column(row):
+    n = row.shape[1]
+    return jnp.transpose(jnp.broadcast_to(row, (n, n)))
+
+
+def as_row(column):
+    n = column.shape[0]
+    return jnp.transpose(jnp.broadcast_to(column, (n, n)))[0:1, :]
+
+
+def put3(ext_ref, at, row):
+    high = row.astype(bf16).astype(f32)
+    rest = row - high
+    middle = rest.astype(bf16).astype(f32)
+    ext_ref[at : at + 1, :] = high
+    ext_ref[at + 1 : at + 2, :] = middle
+    ext_ref[at + 2 : at + 3, :] = rest - middle
+
+
+def get3(ext, at):
+    return ext[at : at + 1, :] + ext[at + 1 : at + 2, :] + ext[at + 2 : at + 3, :]
+
+
+def whole_spec(x):
+    return pl.BlockSpec(x.shape, lambda i: (0,) * len(x.shape))
+
+
+def smem_spec():
+    return pl.BlockSpec(memory_space=pltpu.SMEM)
+
+
+def any_specs(arrays):
+    return [pl.BlockSpec(memory_space=pl.ANY)] * len(arrays)
+
+
+def params(mib=16, **kw):
+    return pltpu.CompilerParams(vmem_limit_bytes=mib * MIB, **kw)
+
+
+def cost(us):
+    return pl.CostEstimate(flops=int(us * 1.1e9), bytes_accessed=0, transcendentals=0)
+
+
+def slots_all(mp_count):
+    return [
+        [("own", z), (z // 2, z % 2), (2 + z, 0), (2 + z, 1), (6 + z // 2, z % 2)] for z in range(mp_count)
+    ]
+
+
+def place_of(r, k):
+    if r < 2:
+        return (2 * r + k, 1)
+    if r < 6:
+        return (r - 2, 2 + k)
+    return (2 * (r - 6) + k, 4)
+
+
+def score_body(rels, indices, slots, rows, tab_ref, eq_ref, *refs):
+    mp_count = len(slots)
+    sources = {}
+    for i, r in enumerate(rels):
+        found = zip(refs[2 * i : 2 * i + 2], indices[2 * i : 2 * i + 2])
+        sources[r] = [ref if index is None else ref.at[index] for ref, index in found]
+    ext_ref = refs[-1]
+    hold = refs[-2]
+    z = tab_ref[32]
+    ext_ref[...] = jnp.zeros_like(ext_ref)
+    for owner, mine in enumerate(slots):
+        target = owner ^ z
+        for i, slot in enumerate(mine):
+            if slot[0] == "own":
+                found = sources[0]
+                lid = qb = slot[1]
+            else:
+                r, k = slot
+                found = sources[r]
+                qb, lid = tab_ref[2 * r + k], tab_ref[16 + 2 * r + k]
+            eq = eq_ref[pl.ds(qb * rows, rows), :]
+            table = p_sq = 0.0
+            for j, ref in enumerate(found):
+                ep = ref[pl.ds(lid * rows, rows), :]
+                width = ep.shape[1]
+                table += mm(ep, eq[:, j * width : (j + 1) * width], NT)
+                ep = ep.astype(f32)
+                p_sq += jnp.sum(ep * ep, axis=1, keepdims=True)
+            q32 = eq.astype(f32)
+            q_sq = jnp.sum(q32 * q32, axis=1, keepdims=True)
+            put3(ext_ref, 0, as_row(q_sq))
+            put3(ext_ref, 3, as_row(p_sq))
+            hold[target, i, :rows, :] = table.astype(bf16)
+            hold[target, i, rows:, :] = ext_ref[...].astype(bf16)
+    outs = refs[-2 - mp_count : -2]
+    for k in range(mp_count):
+        outs[k][...] = hold[k]
+
+
+def score_call(rels, slots, rows, tab, eq, sources, after):
+    mp_count, n = len(slots), len(slots[0])
+    pairs = [pair for r in rels for pair in sources[r]]
+    shape = (n, rows + EXT, rows)
+    outs = [jax.ShapeDtypeStruct(shape, bf16)] * mp_count
+    return pl.pallas_call(
+        functools.partial(score_body, rels, [i for _, i in pairs], slots, rows),
+        out_shape=outs,
+        grid=(1,),
+        in_specs=[smem_spec(), whole_spec(eq)] + [whole_spec(a) for a, _ in pairs] + any_specs(after),
+        out_specs=[whole_spec(o) for o in outs],
+        scratch_shapes=[pltpu.VMEM((mp_count,) + shape, bf16), pltpu.VMEM((EXT, rows), f32)],
+        compiler_params=params(),
+        cost_estimate=cost(4),
+        name="scores",
+    )(tab, eq, *[a for a, _ in pairs], *after)
+
+
+def exp_body(slots, rows, tab_ref, pos_ref, *refs):
+    parts, out, ext_ref = refs[:-2], refs[-2], refs[-1]
+    z = tab_ref[32]
+    ext_ref[...] = jnp.zeros_like(ext_ref)
+    for i, slot in enumerate(slots[0]):
+        total = parts[0][i].astype(f32)
+        for part in parts[1:]:
+            total = total + part[i].astype(f32)
+        ext = total[rows:, :]
+        q_sq, p_sq = get3(ext, 0), get3(ext, 3)
+        q_inv = lax.rsqrt(q_sq + epsilon)
+        p_inv = lax.rsqrt(p_sq + epsilon)
+        scores = total[:rows, :] * as_column(p_inv) * q_inv * (1.0 / logit_divisor)
+        powers = jnp.exp(scores)
+        put3(ext_ref, 0, jnp.sum(powers, axis=0, keepdims=True))
+        put3(ext_ref, 3, jnp.sum(powers * scores, axis=0, keepdims=True))
+        put3(ext_ref, 6, q_sq)
+        put3(ext_ref, 9, p_sq)
+        if slot[0] == "own":
+            match = lax.broadcasted_iota(jnp.int32, (rows, rows), 0) == pos_ref[pl.ds(z, 1), :]
+            put3(ext_ref, 12, jnp.sum(jnp.where(match, powers, 0.0), axis=0, keepdims=True))
+        out[i, :rows, :] = powers.astype(bf16)
+        out[i, rows:, :] = ext_ref[...].astype(bf16)
+
+
+def exp_call(slots, rows, tab, pos, parts):
+    shape = parts[0].shape
+    return pl.pallas_call(
+        functools.partial(exp_body, slots, rows),
+        out_shape=jax.ShapeDtypeStruct(shape, bf16),
+        grid=(1,),
+        in_specs=[smem_spec(), whole_spec(pos)] + [whole_spec(a) for a in parts],
+        out_specs=pl.BlockSpec(shape, lambda i: (0, 0, 0)),
+        scratch_shapes=[pltpu.VMEM((EXT, rows), f32)],
+        compiler_params=params(),
+        cost_estimate=cost(1),
+        name="powers",
+    )(tab, pos, *parts)
+
+
+def totals_of(mp_count, tab_ref, z, hold, tables, tot, inner, q_sq, e_pos):
+    for k in range(mp_count):
+        hold[k] = tables[k][...]
+    tot[...] = jnp.zeros_like(tot)
+    inner[...] = jnp.zeros_like(inner)
+    for owner, slots in enumerate(slots_all(mp_count)):
+        for i, slot in enumerate(slots):
+            ext = hold[owner ^ z, i, hold.shape[2] - EXT :, :].astype(f32)
+            if slot[0] == "own":
+                qb = slot[1]
+                q_sq[qb : qb + 1, :] = get3(ext, 6)
+                e_pos[qb : qb + 1, :] = get3(ext, 12)
+            else:
+                qb = tab_ref[2 * slot[0] + slot[1]]
+            tot[pl.ds(qb, 1), :] += get3(ext, 0)
+            inner[pl.ds(qb, 1), :] += get3(ext, 3)
+
+
+def back_body(to_query, indices, after_count, mp_count, rows, block_count, tab_ref, pos_ref, eq_ref, *refs):
+    dp_count = 8
+    tables, refs = refs[:mp_count], refs[mp_count:]
+    own = refs[:2]
+    halves = {}
+    for r in range(dp_count):
+        found = zip(refs[2 + 2 * r : 4 + 2 * r], indices[2 * r : 2 * r + 2])
+        halves[r] = [ref if index is None else ref.at[0] for ref, index in found]
+    refs = refs[2 + 2 * dp_count + after_count :]
+    if to_query:
+        dq_outs, loss_out = refs[:2], refs[2]
+        refs = refs[3:]
+    else:
+        own_out, c_outs = refs[0], refs[1 : 1 + dp_count // 2]
+        refs = refs[1 + dp_count // 2 :]
+    hold, refs = refs[0], refs[1:]
+    tot, inner, q_sq, e_pos = refs[:4]
+    z = tab_ref[32]
+    step = pl.program_id(0)
+    half = own[0].shape[1]
+
+    @pl.when(step == 0)
+    def _():
+        totals_of(mp_count, tab_ref, z, hold, tables, tot, inner, q_sq, e_pos)
+        if to_query:
+            refs[4][...] = jnp.zeros_like(refs[4])
+            positive = jnp.log(e_pos[...])
+            loss_out[...] = jnp.log(tot[...]) - positive
+            inner[...] = inner[...] / tot[...] - positive
+
+    def visit(place, sources, at, qb, is_own, out_ref=None):
+        owner, i = place
+        ext = hold[owner ^ z, i, rows:, :].astype(f32)
+        powers = hold[owner ^ z, i, :rows, :].astype(f32)
+        p_inv = as_column(lax.rsqrt(get3(ext, 9) + epsilon))
+        total = tot[pl.ds(qb, 1), :]
+        weight = powers * (1.0 / total)
+        if is_own:
+            match = lax.broadcasted_iota(jnp.int32, (rows, rows), 0) == pos_ref[pl.ds(qb, 1), :]
+            weight = jnp.where(match, e_pos[pl.ds(qb, 1), :] / total - 1.0, weight)
+        to_q = weight * (p_inv * (1.0 / logit_divisor))
+        rows_of_q = pl.ds(qb * rows, rows)
+        if to_query:
+            to_q = to_q.astype(bf16)
+            for j, ref in enumerate(sources):
+                refs[4][rows_of_q, j * half : (j + 1) * half] += mm(to_q, ref[at, :], TN)
+            return
+        p_inner = jnp.sum(weight * jnp.log(powers), axis=1, keepdims=True)
+        to_p = (to_q * lax.rsqrt(get3(ext, 6) + epsilon)).astype(bf16)
+        factor = p_inner * p_inv[:, 0:1] * p_inv[:, 0:1]
+        for j, ref in enumerate(sources):
+            cols = slice(j * half, (j + 1) * half)
+            back = mm(to_p, eq_ref[rows_of_q, cols], NN) - ref[at, :].astype(f32) * factor
+            out_ref[:, cols] = back.astype(bf16)
+
+    per_step = block_count // 2
+    for r in reversed(range(dp_count)):
+        out = () if to_query else (c_outs[r // 2].at[r % 2, 0],)
+        visit(place_of(r, step), halves[r], pl.ds(0, rows), tab_ref[2 * r + step], False, *out)
+    for j in range(per_step):
+        b = step * per_step + j
+        out = () if to_query else (own_out.at[j],)
+        visit((b, 0), own, pl.ds(j * rows, rows), b, True, *out)
+
+    if to_query:
+
+        @pl.when(step == 1)
+        def _():
+            for b in range(block_count):
+                q_inv = as_column(lax.rsqrt(q_sq[b : b + 1, :] + epsilon))[:, 0:1]
+                q_inner = as_column(inner[b : b + 1, :])[:, 0:1]
+                at = slice(b * rows, (b + 1) * rows)
+                out = refs[4][at, :] * q_inv - eq_ref[at, :].astype(f32) * (q_inv * q_inv * q_inner)
+                dq_outs[b // per_step][(b % per_step) * rows : (b % per_step + 1) * rows, :] = out.astype(bf16)
+
+
+def back_call(to_query, mp_count, rows, block_count, tab, pos, eq, tables, sources, after=()):
+    dp_count = 8
+    width = eq.shape[1]
+    half = width // 2
+    whole = lambda shape: pl.BlockSpec(shape, lambda k, tab: (0,) * len(shape))
+    table_specs = [whole(t.shape) for t in tables]
+    per_step = block_count // 2
+    own_specs = [pl.BlockSpec((per_step * rows, half), lambda k, tab: (k, 0))] * 2
+
+    def half_spec(r, index):
+        if index is None:
+            return pl.BlockSpec((rows, half), lambda k, tab: (tab[16 + 2 * r + k], 0))
+        return pl.BlockSpec((1, rows, half), lambda k, tab: (index, tab[16 + 2 * r + k], 0))
+
+    pairs = [pair for r in range(dp_count) for pair in sources[r]]
+    half_specs = [half_spec(r, index) for r in range(dp_count) for _, index in sources[r]]
+    c_spec = pl.BlockSpec((2, 1, rows, width), lambda k, tab: (0, k, 0, 0))
+    scratch = [pltpu.VMEM((mp_count,) + tables[0].shape, bf16)]
+    scratch += [pltpu.VMEM((block_count, rows), f32)] * 4
+    part = (per_step * rows, width)
+    if to_query:
+        out_specs = [whole(part), whole(part), whole((block_count, rows))]
+        out_shape = [jax.ShapeDtypeStruct(part, bf16)] * 2 + [jax.ShapeDtypeStruct((block_count, rows), f32)]
+        scratch += [pltpu.VMEM(eq.shape, f32)]
+    else:
+        out_specs = [pl.BlockSpec((per_step, rows, width), lambda k, tab: (k, 0, 0))] + [c_spec] * (dp_count // 2)
+        out_shape = [jax.ShapeDtypeStruct((block_count, rows, width), bf16)]
+        out_shape += [jax.ShapeDtypeStruct((2, 2, rows, width), bf16)] * (dp_count // 2)
+    grid_spec = pltpu.PrefetchScalarGridSpec(
+        num_scalar_prefetch=1,
+        grid=(2,),
+        in_specs=[whole(pos.shape), whole(eq.shape)]
+        + table_specs
+        + own_specs
+        + half_specs
+        + any_specs(after),
+        out_specs=out_specs,
+        scratch_shapes=scratch,
+    )
+    return pl.pallas_call(
+        functools.partial(back_body, to_query, [i for _, i in pairs], len(after), mp_count, rows, block_count),
+        grid_spec=grid_spec,
+        out_shape=out_shape,
+        compiler_params=params(50, dimension_semantics=("arbitrary",)),
+        cost_estimate=cost(6),
+        name="query_gradient" if to_query else "passage_terms",
+    )(
+        tab,
+        pos,
+        eq,
+        *tables,
+        *[a for a, _ in sources[0]],
+        *[a for a, _ in pairs],
+        *after,
+    )
+
+
+def gather_body(rows, block_count, count, tab_ref, own_ref, *refs):
+    arrived, outs, acc = refs[:count], refs[-3:-1], refs[-1]
+    for b in range(block_count):
+        acc[b * rows : (b + 1) * rows, :] = own_ref[b].astype(f32)
+    for r, ref in enumerate(arrived):
+        for k in range(2):
+            at = pl.ds(tab_ref[2 * (tab_ref[16] ^ r) + k] * rows, rows)
+            acc[at, :] += ref[0, k].astype(f32)
+    part = outs[0].shape[0]
+    for j in range(2):
+        outs[j][...] = acc[j * part : (j + 1) * part, :].astype(bf16)
+
+
+def gather_call(rows, block_count, tab, own, arrived, after):
+    width = own.shape[2]
+    part = (block_count * rows // 2, width)
+    return pl.pallas_call(
+        functools.partial(gather_body, rows, block_count, len(arrived)),
+        out_shape=[jax.ShapeDtypeStruct(part, bf16)] * 2,
+        grid=(1,),
+        in_specs=[smem_spec(), whole_spec(own)] + [pl.BlockSpec((1,) + a.shape[1:], lambda i, k=k: (k,) + (0,) * (a.ndim - 1)) for a, k in arrived] + any_specs(after),
+        out_specs=[pl.BlockSpec(part, lambda i: (0, 0))] * 2,
+        scratch_shapes=[pltpu.VMEM((block_count * rows, width), f32)],
+        compiler_params=params(),
+        cost_estimate=cost(3),
+        name="sum_returned",
+    )(tab, own, *[a for a, _ in arrived], *after)
+
+
+def pack_body(count, *refs):
+    for i in range(count):
+        refs[-1][i] = refs[i][0]
+
+
+def pack(parts, after):
+    shape = parts[0].shape[1:]
+    zeros = (0,) * len(shape)
+    return pl.pallas_call(
+        functools.partial(pack_body, len(parts)),
+        grid=(1,),
+        out_shape=jax.ShapeDtypeStruct((len(parts),) + shape, parts[0].dtype),
+        in_specs=[pl.BlockSpec((1,) + shape, lambda i: (1,) + zeros)] * len(parts) + any_specs(after),
+        out_specs=pl.BlockSpec((len(parts),) + shape, lambda i: (0,) + zeros),
+        compiler_params=params(),
+        cost_estimate=cost(2),
+        name="pack",
+    )(*parts, *after)
+
+
+def slab_sum(hidden_ref, top_ref, bottom_ref):
+    part = top_ref.shape[0]
+    return mm(hidden_ref[:part, :], top_ref[...], TN) + mm(hidden_ref[part:, :], bottom_ref[...], TN)
+
+
+def slabs_body(has_earlier, tab_ref, hidden_ref, top_ref, bottom_ref, *refs):
+    out = slab_sum(hidden_ref, top_ref, bottom_ref)
+    if has_earlier:
+        out = out + refs[0][0].astype(f32)
+    refs[-1][0] = out.astype(bf16)
+
+
+def home_body(tab_ref, hidden_ref, top_ref, bottom_ref, earlier_ref, arrived_ref, *outs):
+    out = slab_sum(hidden_ref, top_ref, bottom_ref) + earlier_ref[0].astype(f32) + arrived_ref[0].astype(f32)
+    half = out.shape[1] // 2
+    out = out.astype(bf16)
+    g = pl.program_id(0)
+    for j, early in enumerate((g < 2, (g == 0) | (g == 2))):
+
+        @pl.when(early)
+        def _():
+            outs[2 * j][0] = out[:, j * half : (j + 1) * half]
+
+        @pl.when(jnp.logical_not(early))
+        def _():
+            outs[2 * j + 1][0] = out[:, j * half : (j + 1) * half]
+
+
+def weight_slabs(order, me, hidden, d, earlier=None, arrived=None, after=()):
+    count, depth = hidden.shape[1] // 8, hidden.shape[0]
+    part, width = d[0].shape
+    targets = jnp.stack([me ^ r for r in order]).astype(jnp.int32)
+    whole = pl.BlockSpec((part, width), lambda i, tab: (0, 0))
+    in_specs = [pl.BlockSpec((depth, count), lambda i, tab: (0, tab[i])), whole, whole]
+    slab = pl.BlockSpec((1, count, width), lambda i, tab: (i, 0, 0))
+    more = [a for a in (earlier, arrived) if a is not None]
+    if arrived is None:
+        body, out_specs = functools.partial(slabs_body, earlier is not None), slab
+        out_shape = jax.ShapeDtypeStruct((len(order), count, width), bf16)
+    else:
+        body = home_body
+        piece = (1, count, width // 2)
+        out_specs = [
+            pl.BlockSpec(piece, lambda i, tab: (jnp.minimum(i, 1), 0, 0)),
+            pl.BlockSpec(piece, lambda i, tab: (jnp.maximum(i - 2, 0), 0, 0)),
+            pl.BlockSpec(piece, lambda i, tab: (jnp.minimum(i // 2, 1), 0, 0)),
+            pl.BlockSpec(piece, lambda i, tab: (jnp.where(i == 3, 1, 0), 0, 0)),
+        ]
+        out_shape = [jax.ShapeDtypeStruct((2, count, width // 2), bf16)] * 4
+    return pl.pallas_call(
+        body,
+        grid_spec=pltpu.PrefetchScalarGridSpec(
+            num_scalar_prefetch=1, grid=(len(order),), in_specs=in_specs + [slab] * len(more) + any_specs(after), out_specs=out_specs
+        ),
+        out_shape=out_shape,
+        compiler_params=params(dimension_semantics=("arbitrary",)),
+        cost_estimate=cost(4 if arrived is None else 5),
+        name="weight_slabs",
+    )(targets, hidden, *d, *more, *after)
+
+
+def add_body(a_ref, b_ref, out_ref):
+    out_ref[...] = (a_ref[...].astype(f32) + b_ref[...].astype(f32)).astype(bf16)
+
+
+def add_halves(first, second):
+    def body(a_ref, b_ref, c_ref, d_ref, left_ref, right_ref):
+        add_body(a_ref.at[0], b_ref.at[0], left_ref)
+        add_body(c_ref.at[0], d_ref.at[0], right_ref)
+
+    shape = first[0].shape[1:]
+    block = pl.BlockSpec((1,) + shape, lambda i: (0, 0, 0))
+    out = pl.BlockSpec(shape, lambda i: (0, 0))
+    return pl.pallas_call(
+        body,
+        grid=(1,),
+        in_specs=[block] * 4,
+        out_specs=[out] * 2,
+        out_shape=[jax.ShapeDtypeStruct(shape, bf16)] * 2,
+        compiler_params=params(),
+        cost_estimate=cost(1.4),
+        name="add_halves",
+    )(*first, *second)
+
+
+def last_sum_body(left_ref, xa_ref, ya_ref, right_ref, yb_ref, xb_ref, out_ref):
+    half = ya_ref.shape[1]
+    for j, (mine, first, second) in enumerate(((left_ref, xa_ref, ya_ref), (right_ref, yb_ref, xb_ref))):
+        total = mine[0].astype(f32) + first[0].astype(f32) + second[...].astype(f32)
+        out_ref[:, j * half : (j + 1) * half] = total
+
+
+def last_sum(left, xa, ya, right, yb, xb):
+    rows, half = ya.shape
+    tile = rows // 4
+    block = pl.BlockSpec((1, tile, half), lambda i: (1, i, 0))
+    flat = pl.BlockSpec((tile, half), lambda i: (i, 0))
+    return pl.pallas_call(
+        last_sum_body,
+        grid=(4,),
+        in_specs=[block, block, flat] * 2,
+        out_specs=pl.BlockSpec((tile, 2 * half), lambda i: (i, 0)),
+        out_shape=jax.ShapeDtypeStruct((rows, 2 * half), f32),
+        compiler_params=params(dimension_semantics=("arbitrary",)),
+        cost_estimate=cost(3),
+        name="last_sum",
+    )(left, xa, ya, right, yb, xb)
+
+
+def stack_body(count, *refs):
+    for i in range(count):
+        refs[-1][i] = refs[i][...]
+
+
+def stack(parts, after):
+    return pl.pallas_call(
+        functools.partial(stack_body, len(parts)),
+        out_shape=jax.ShapeDtypeStruct((len(parts),) + parts[0].shape, parts[0].dtype),
+        grid=(1,),
+        in_specs=[whole_spec(a) for a in parts] + any_specs(after),
+        out_specs=pl.BlockSpec((len(parts),) + parts[0].shape, lambda i: (0,) * (1 + parts[0].ndim)),
+        compiler_params=params(),
+        cost_estimate=cost(1),
+        name="stack",
+    )(*parts, *after)
+
+
+def slab_body(mp_count, tab_ref, start_ref, *refs):
+    count = mp_count - 1
+    inner, outer = refs[:count], refs[count : 2 * count - 1]
+    weight_ref, out_ref, held = refs[2 * count - 1 :]
+    z = tab_ref[0]
+
+    @pl.when(pl.program_id(0) == 0)
+    def _():
+        for k in range(1, mp_count):
+            source = z ^ k
+            by_partner = (source > z) == (z % 2 == 0)
+            steps = jnp.abs(source - z)
+            for u in range(1, mp_count):
+
+                @pl.when(by_partner & (steps == u))
+                def _():
+                    held[k - 1] = inner[u - 1][...]
+
+                if u < mp_count - 1:
+
+                    @pl.when(jnp.logical_not(by_partner) & (steps == u))
+                    def _():
+                        held[k - 1] = outer[u - 1][...]
+
+    out = start_ref[...]
+    for k in range(count):
+        shares_of = weight_ref[:, pl.ds(z ^ (k + 1), 1)]
+        out = out + mm(held[k], shares_of.reshape(-1, shares_of.shape[-1]), NT)
+    out_ref[...] = out.astype(bf16)
+
+
+def slab_product(z, mp_count, start, inner, outer, weights):
+    depth, width = start.shape
+    tile = width // 4
+    tab = z[None].astype(jnp.int32)
+    rows = pl.BlockSpec(inner[0].shape, lambda g, tab: (0, 0))
+    block = pl.BlockSpec((depth, tile), lambda g, tab: (0, g))
+    return pl.pallas_call(
+        functools.partial(slab_body, mp_count),
+        grid_spec=pltpu.PrefetchScalarGridSpec(
+            num_scalar_prefetch=1,
+            grid=(4,),
+            in_specs=[block]
+            + [rows] * (len(inner) + len(outer))
+            + [pl.BlockSpec((weights.shape[0] // 4,) + weights.shape[1:], lambda g, tab: (g, 0, 0, 0))],
+            out_specs=block,
+            scratch_shapes=[pltpu.VMEM((mp_count - 1,) + inner[0].shape, bf16)],
+        ),
+        out_shape=jax.ShapeDtypeStruct(start.shape, bf16),
+        compiler_params=params(dimension_semantics=("arbitrary",)),
+        cost_estimate=cost(4),
+        name="slab_product",
+    )(tab, start, *inner, *outer, weights)
+
+
+def xor_pairs(count, mask):
+    return [(i, i ^ mask) for i in range(count)]
+
+
+def parts_body(count, after_count, tab_ref, top_ref, bottom_ref, weight_ref, *refs):
+    k = pl.program_id(0)
+    refs[after_count][0] = mm(top_ref[...], weight_ref[...], NT).astype(bf16)
+    if count > 1:
+
+        @pl.when(k == count - 1)
+        def _():
+            refs[-1][...] = mm(bottom_ref[...], weight_ref[...], NT)
+
+
+def line_parts(d, weight, slabs, after=()):
+    top, bottom = d
+    rows, width = top.shape
+    slab = weight.shape[0] // 4
+    count = len(slabs)
+    tab = jnp.stack(slabs).astype(jnp.int32)
+    whole = pl.BlockSpec((rows, width), lambda k, tab: (0, 0))
+    more = 1 if count > 1 else 0
+    return pl.pallas_call(
+        functools.partial(parts_body, count, len(after)),
+        grid_spec=pltpu.PrefetchScalarGridSpec(
+            num_scalar_prefetch=1,
+            grid=(count,),
+            in_specs=[whole, whole, pl.BlockSpec((slab, width), lambda k, tab: (tab[k], 0))] + any_specs(after),
+            out_specs=[pl.BlockSpec((1, rows, slab), lambda k, tab: (k, 0, 0))]
+            + [pl.BlockSpec((rows, slab), lambda k, tab: (0, 0))] * more,
+        ),
+        out_shape=[jax.ShapeDtypeStruct((count, rows, slab), bf16)] + [jax.ShapeDtypeStruct((rows, slab), f32)] * more,
+        compiler_params=params(dimension_semantics=("arbitrary",)),
+        cost_estimate=cost(1 + count),
+        name="line_parts",
+    )(tab, top, bottom, weight, *after)
+
+
+def pass_body(masks, after_count, tab_ref, *refs):
+    n = len(masks)
+    z = tab_ref[0]
+    at_end = (z == 0) | (z == 3)
+    for got, part, out, mask in zip(refs[:n], refs[n : 2 * n], refs[2 * n + after_count :], masks):
+        term = part[0].astype(f32)
+        if mask == "ends":
+            term = jnp.where(at_end, term, 0.0)
+        elif mask == "middle":
+            term = jnp.where(at_end, 0.0, term)
+        out[...] = (got[...].astype(f32) + term).astype(bf16)
+
+
+def pass_on(z, *jobs, after=()):
+    shape = jobs[0][0].shape
+    whole = pl.BlockSpec(shape, lambda i: (0, 0))
+    part_specs = [pl.BlockSpec((1,) + shape, lambda i, k=job[2]: (k, 0, 0)) for job in jobs]
+    return pl.pallas_call(
+        functools.partial(pass_body, [job[3] for job in jobs], len(after)),
+        grid=(1,),
+        in_specs=[smem_spec()] + [whole] * len(jobs) + part_specs + any_specs(after),
+        out_specs=[whole] * len(jobs),
+        out_shape=[jax.ShapeDtypeStruct(shape, bf16)] * len(jobs),
+        compiler_params=params(),
+        cost_estimate=cost(1.5),
+        name="pass_on",
+    )(z[None].astype(jnp.int32), *[job[0] for job in jobs], *[job[1] for job in jobs], *after)
+
+
+def line_start(d, weight, z, mp_count):
+    (first,) = line_parts(d, weight, [z ^ 3])
+    return [lax.ppermute(d[1], "mp", xor_pairs(mp_count, 1))], [lax.ppermute(d[1], "mp", [(1, 2), (2, 1)])], first
+
+
+def line_steps(d, weight, z, mp_count, begun, before_parts=(), before_third=()):
+    inner, outer, first = begun
+    inner_swap = lambda a: lax.ppermute(a, "mp", xor_pairs(mp_count, 1))
+    outer_swap = lambda a: lax.ppermute(a, "mp", [(1, 2), (2, 1)])
+    (to_inner,) = pass_on(z, (outer[0], first, 0, "ends"), after=before_parts)
+    to_outer = inner[0]
+    parts, own_bottom = line_parts(d, weight, [z ^ 2, z ^ 1, z], (to_inner,))
+    inner, outer, sent = inner + [inner_swap(to_inner)], outer + [outer_swap(to_outer)], []
+    to_inner, to_outer = pass_on(z, (outer[1], parts, 0, "ends"), (inner[1], parts, 0, "middle"), after=before_third)
+    sent.append(to_inner)
+    inner, outer = inner + [inner_swap(to_inner)], outer + [outer_swap(to_outer)]
+    to_inner, to_outer = pass_on(z, (outer[2], parts, 1, "all"), (inner[2], first, 0, "middle"))
+    sent.append(to_inner)
+    inner, outer = inner + [inner_swap(to_inner)], outer + [outer_swap(to_outer)]
+    return parts, own_bottom, inner, outer, sent
+
+
+def line_bottom(z, mp_count, begun, weights):
+    _, own_bottom, inner, outer, _ = begun
+    return slab_product(z, mp_count, own_bottom, inner[:3], outer[:2], weights)
+
+
+def line_finish(begun, bottom):
+    parts, _, inner, outer, _ = begun
+    return joined(parts, inner[3], outer[3], bottom)
+
+
+def joined_body(part_ref, a_ref, b_ref, bottom_ref, out_ref):
+    rows = a_ref.shape[0]
+    total = part_ref[0].astype(f32) + a_ref[...].astype(f32) + b_ref[...].astype(f32)
+    out_ref[:rows, :] = total.astype(bf16)
+    out_ref[rows:, :] = bottom_ref[...]
+
+
+def joined(parts, a, b, bottom):
+    rows, width = a.shape
+    whole = pl.BlockSpec((rows, width), lambda i: (0, 0))
+    return pl.pallas_call(
+        joined_body,
+        grid=(1,),
+        in_specs=[pl.BlockSpec((1, rows, width), lambda i: (2, 0, 0)), whole, whole, whole],
+        out_specs=pl.BlockSpec((2 * rows, width), lambda i: (0, 0)),
+        out_shape=jax.ShapeDtypeStruct((2 * rows, width), bf16),
+        compiler_params=params(),
+        cost_estimate=cost(1.2),
+        name="joined",
+    )(parts, a, b, bottom)
+
+
+def slots_of(ids, rel):
+    place = jnp.arange(ids.shape[-1], dtype=jnp.int32)
+    earlier = (rel[..., :, None] == rel[..., None, :]) & (place[None, :] < place[:, None])
+    return rel * 2 + jnp.sum(earlier.astype(jnp.int32), axis=-1)
+
+
+def tables_of(neg_blocks, me, z, dp_count, block_count):
+    wanted = neg_blocks.reshape(-1)
+    count = wanted.shape[0]
+    neg_count = count // block_count
+    place = jnp.arange(count, dtype=jnp.int32)
+    slot = slots_of(wanted, (wanted // block_count) ^ me)
+    hot = (slot[:, None] == place[None, :]).astype(jnp.int32)
+    query_of = jnp.sum(hot * (place // neg_count)[:, None], axis=0)
+    local_of = jnp.sum(hot * (wanted % block_count)[:, None], axis=0)
+    tab = jnp.concatenate([query_of, local_of, z[None]]).astype(jnp.int32)
+    rows_of = (wanted // block_count)[None, :] == jnp.arange(dp_count, dtype=jnp.int32)[:, None]
+    rank = jnp.sum((rows_of[:, :, None] & (place[None, :, None] < place[None, None, :])).astype(jnp.int32), axis=1)
+    local = jnp.where(rows_of, wanted % block_count, 0)
+    asks = jnp.stack([jnp.sum(jnp.where(rank == k, local, 0), axis=1) for k in range(2)], axis=1)
+    asked = lax.all_to_all(asks, "dp", 0, 0, tiled=True).reshape(-1)
+    return tab, jnp.concatenate([asked, me[None]]).astype(jnp.int32)
+
+
+def neighbours(query_hidden, passage_hidden, head_weight, neg_blocks, pos_ids):
+    dp_count, mp_count = lax.axis_size("dp"), lax.axis_size("mp")
+    me, z = lax.axis_index("dp"), lax.axis_index("mp")
+    block_count = neg_blocks.shape[0]
+    rows = query_hidden.shape[0] // block_count
+    width = head_weight.shape[1]
+    half = width // 2
+    swap = lambda a, mask: lax.ppermute(a, "dp", xor_pairs(dp_count, mask))
+    across = lambda a, mask: lax.ppermute(a, "mp", xor_pairs(mp_count, mask))
+
+    slab = head_weight.shape[0] // mp_count
+    share = lax.dynamic_index_in_dim(head_weight.reshape(mp_count, dp_count, slab // dp_count, width), me, 1, False)
+    share = lax.all_to_all(share, "mp", 0, 0, tiled=True)
+    ea = mm(passage_hidden, head_weight[:, :half], NN).astype(bf16)
+    eb = mm(passage_hidden, head_weight[:, half:], NN).astype(bf16)
+    eq = mm(query_hidden, head_weight, NN).astype(bf16)
+    ax, by = swap(ea, 2), swap(eb, 4)
+    ay, bx = swap(ea, 4), swap(eb, 2)
+    ad, bd = swap(ax, 4), swap(by, 2)
+    core = swap(stack([ea, eb], ()), 1)
+    core_xy = swap(stack([ax, bx, ay, by], ()), 1)
+    core_d = swap(stack([ad, bd], (eq,)), 1)
+    sources = {
+        0: [(ea, None), (eb, None)],
+        1: [(core, 0), (core, 1)],
+        2: [(ax, None), (bx, None)],
+        3: [(core_xy, 0), (core_xy, 1)],
+        4: [(ay, None), (by, None)],
+        5: [(core_xy, 2), (core_xy, 3)],
+        6: [(ad, None), (bd, None)],
+        7: [(core_d, 0), (core_d, 1)],
+    }
+    tab, asked = tables_of(neg_blocks, me, z, dp_count, block_count)
+    pos = pos_ids.reshape(block_count, rows)
+    slots = slots_all(mp_count)
+    sent = score_call(tuple(range(dp_count)), slots, rows, tab, eq, sources, ())
+    parts = [sent[0]] + [across(sent[k], k) for k in range(1, mp_count)]
+    mine = exp_call(slots, rows, tab, pos, parts)
+    tables = [mine] + [across(mine, k) for k in range(1, mp_count)]
+    weights = lax.all_gather(stack([share], (sent[0],))[0], "dp", axis=0)
+
+    *dq, loss = back_call(True, mp_count, rows, block_count, tab, pos, eq, tables, sources)
+    query_begun = line_start(dq, head_weight, z, mp_count)
+    own, here, to_x, to_y, to_d = back_call(
+        False, mp_count, rows, block_count, tab, pos, eq, tables, sources, (query_begun[-1],)
+    )
+    query_line = line_steps(dq, head_weight, z, mp_count, query_begun, (here,))
+    away, home = (7, 3, 5, 1), (6, 2, 4, 0)
+    away_q = weight_slabs(away, me, query_hidden, dq)
+    home_q = weight_slabs(home, me, query_hidden, dq)
+    query_bottom = line_bottom(z, mp_count, query_line, weights)
+    got = [swap(to_x, 2), swap(to_y, 4), swap(to_d, 6)]
+    other = swap(pack([here] + got, query_line[-1] + [away_q, home_q, asked, query_bottom]), 1)
+    arrived = {}
+    for i, a in enumerate([here] + got):
+        arrived[2 * i], arrived[2 * i + 1] = (a, 0), (other, i)
+    dp = gather_call(
+        rows,
+        block_count,
+        asked,
+        own,
+        [arrived[r] for r in range(dp_count)],
+        [query_line[2][-1], query_line[3][-1]],
+    )
+    passage_begun = line_start(dp, head_weight, z, mp_count)
+    away_sum = weight_slabs(away, me, passage_hidden, dp, away_q, None, (passage_begun[-1],))
+    query_grad = line_finish(query_line, query_bottom)
+    passage_line = line_steps(dp, head_weight, z, mp_count, passage_begun, (away_sum,), (query_grad,))
+    left, left_more, right, right_more = weight_slabs(home, me, passage_hidden, dp, home_q, swap(away_sum, 1))
+    xa, yb = swap(left, 2), swap(right, 4)
+    to_y, to_x = add_halves((left_more, xa), (right_more, yb))
+    grad_weight = last_sum(left_more, xa, swap(to_y, 4), right_more, yb, swap(to_x, 2))
+    passage_grad = line_finish(passage_line, line_bottom(z, mp_count, passage_line, weights))
+    return loss.reshape(-1), grad_weight, query_grad, passage_grad
 
 
 def back_norm(inverse, unit_rows, d_unit, inner):
     return (inverse[:, None] * (d_unit - unit_rows * inner[:, None])).astype(jnp.bfloat16)
 
 
-def local(query_hidden, passage_hidden, head_weight, neg_blocks, pos_ids):
+def general(query_hidden, passage_hidden, head_weight, neg_blocks, pos_ids):
     dp_count = lax.axis_size("dp")
     block_count, neg_count = neg_blocks.shape
     row_count = query_hidden.shape[0]
@@ -144,6 +916,13 @@
 
 def solution(mesh):
     placed = (P("dp", None), P("dp", None), P(None, "mp"), P("dp", None), P("dp"))
+    sizes = dict(mesh.shape)
+
+    def local(query_hidden, passage_hidden, head_weight, neg_blocks, pos_ids):
+        exact = sizes["dp"] == 8 and sizes["mp"] == 4 and neg_blocks.shape == (4, 4)
+        chosen = neighbours if exact else general
+        return chosen(query_hidden, passage_hidden, head_weight, neg_blocks, pos_ids)
+
     return jax.shard_map(
         local,
         mesh=mesh,

time: 534 us -> 296 us (0.55)
  waiting for transfers between devices: 331 us -> 76.8 us
  Pallas kernels: 0 us -> 69.7 us
  starting transfers between devices: 15.1 us -> 78.2 us
  matrix products: 65.8 us -> 16.9 us
  local copies, waits for them, and re-layouts: 64.7 us -> 37.1 us
  blocking collectives: 22.5 us -> 0 us
  other arithmetic: 20.2 us -> 1.61 us
    reduce_scatter x3 -> x0, waiting for transfers between devices: 203 us -> none  [the longest x1 80 us: local(): lax.psum_scatter(passage_back, 'mp', scatter_dimension=1, tiled=True)]
    all_to_all x3 -> x2, waiting for transfers between devices: 90.7 us -> 0.01 us  [the longest x1 0.01 us: neighbours(): share = lax.all_to_all(share, 'mp', 0, 0, tiled=True)]
    ppermute x0 -> x40, waiting for transfers between devices: none -> 76.8 us  [the longest x6 31.8 us: line_steps(): inner_swap = lambda a: lax.ppermute(a, 'mp', xor_pairs(mp_count, 1))]
    pallas_call x0 -> x30, Pallas kernels: none -> 69.7 us  [the longest x4 15.5 us: weight_slabs(): pl.pallas_call(body, grid_spec=pltpu.PrefetchScalarGridSpec(num_scalar_pr...]
    ppermute x0 -> x40, starting transfers between devices: none -> 69.1 us  [the longest x6 32.7 us: line_steps(): inner_swap = lambda a: lax.ppermute(a, 'mp', xor_pairs(mp_count, 1))]
    dot_general x10 -> x3, matrix products: 65.8 us -> 16.9 us  [mm(): return lax.dot_general(a, b, dims, preferred_element_type=f32)]
    psum x1 -> x0, waiting for transfers between devices: 37 us -> none  [local(): lax.psum(similarity_parts.astype(jnp.bfloat16), 'mp').astype(jnp.float32)]
    psum x2 -> x0, blocking collectives: 22.5 us -> none  [the longest x1 11.9 us: local(): lax.psum((jnp.sum(query_embed * query_embed, axis=1), jnp.sum(passage_emb...]
  transfers between devices with their start and end apart: 7 -> 43, of which waited for: 6 -> 16; matrix products, arithmetic and copies ran while one was open for 8% -> 5% of each run, Pallas kernels for 0% -> 19%
where the time goes in v1:
time: 296 us; the launch traced here: 295 us
  starting transfers between devices  78.2 us (26%)
  waiting for transfers between devices  76.8 us (26%)
  Pallas kernels  69.7 us (24%)
  local copies, waits for them, and re-layouts  37.1 us (13%)
  matrix products  16.9 us (6%)
  between operations  14.7 us (5%)
    unnamed x132, local copies, waits for them, and re-layouts  33.5 us
    ppermute x6, starting transfers between devices, line_steps(): inner_swap = lambda a: lax.ppermute(a, 'mp', xor_pairs(mp_count, 1))  32.7 us
    ppermute x6, waiting for transfers between devices, line_steps(): inner_swap = lambda a: lax.ppermute(a, 'mp', xor_pairs(mp_count, 1))  31.8 us
    ppermute x18, waiting for transfers between devices, neighbours(): swap = lambda a, mask: lax.ppermute(a, 'dp', xor_pairs(dp_count, mask))  23.7 us
    ppermute x6, waiting for transfers between devices, neighbours(): across = lambda a, mask: lax.ppermute(a, 'mp', xor_pairs(mp_count, mask))  21.2 us
    dot_general x3, matrix products, mm(): return lax.dot_general(a, b, dims, preferred_element_type=f32)  16.9 us
    pallas_call x4, Pallas kernels, weight_slabs(): pl.pallas_call(body, grid_spec=pltpu.PrefetchScalarGridSpec(num_scalar_pr...  15.5 us
    ppermute x18, starting transfers between devices, neighbours(): swap = lambda a, mask: lax.ppermute(a, 'dp', xor_pairs(dp_count, mask))  14.9 us
  transfers between devices with their start and end apart: 43, of which 16 were waited for; matrix products, arithmetic and copies ran while one was open for 5% of the time, Pallas kernels for 19%

profile of v1, /device:TPU:0, one launch (start us, length us, event | category | flops | bytes accessed | tf_op | source)
XLA Modules:
  0.0 295.1 jit_solution(3965390440419854381)
XLA Ops:
  7.2 6.7 %fusion.4.refs_0_.refs_4_.refs_6_ = bf16[512,512]{1,0:T(8,128)(2,1)} fusion(bf16[512,4096]{1,0:T(8,128)(2,1)} %hidden_ref.7, bf16[4096,1024]{1,0:T(8,128)(2,1)} %weight_ref.7), kind=kOutput, calls=%fused_computation.5 | convolution fusion | flops 2147745792 | bytes 8912896 | tf_op jit(solution)/shard_map/dot_general | solution.py:22
  24.4 5.4 %all-to-all-start.1 = ((bf16[4,128,1024]{2,1,0:T(8,128)(2,1)}), bf16[4,128,1024]{2,1,0:T(8,128)(2,1)}, u32[]{:S(2)}, u32[]{:S(2)}) async-start(bf16[4,128,1024]{2,1,0:T(8,128)(2,1)} %dynamic-slice_bitcast_fusion), calls=%async_computation.1 | async-start | bytes 2097152 | tf_op jit(solution)/shard_map/all_to_all | solution.py:718
  32.2 8.1 %collective-permute-done.4.refs_3_.refs_9_.refs_15_ = bf16[512,512]{1,0:T(8,128)(2,1)S(1)} collective-permute-done((bf16[512,512]{1,0:T(8,128)(2,1)}, bf16[512,512]{1,0:T(8,128)(2,1)S(1)}, u32[]{:S(2)}, u32[]{:S(2)}) %collective-permute-start.4) | collective-permute-done | bytes 524320 | tf_op jit(solution)/shard_map/ppermute | solution.py:713
  48.5 7.0 %convolution_convert_fusion.refs_2_.eq_ref = bf16[512,1024]{1,0:T(8,128)(2,1)S(1)} fusion(bf16[512,4096]{1,0:T(8,128)(2,1)S(1)} %copy-done.35, bf16[4096,1024]{1,0:T(8,128)(2,1)} %weight_ref.7), kind=kOutput, calls=%fused_computation.4 | convolution fusion | flops 4295491584 | bytes 13631488 | tf_op jit(solution)/shard_map/dot_general | solution.py:22
  55.5 5.5 %collective-permute-done.6.refs_0_.refs_12_.refs_18_ = bf16[512,512]{1,0:T(8,128)(2,1)S(1)} collective-permute-done((bf16[512,512]{1,0:T(8,128)(2,1)}, bf16[512,512]{1,0:T(8,128)(2,1)S(1)}, u32[]{:S(2)}, u32[]{:S(2)}) %collective-permute-start.6) | collective-permute-done | bytes 524320 | tf_op jit(solution)/shard_map/ppermute | solution.py:713
  73.8 6.4 %scores.1 = (bf16[5,144,128]{2,1,0:T(8,128)(2,1)S(1)}, bf16[5,144,128]{2,1,0:T(8,128)(2,1)}, bf16[5,144,128]{2,1,0:T(8,128)(2,1)}, bf16[5,144,128]{2,1,0:T(8,128)(2,1)}) custom-call(s32[33]{0:T(128)S(1)} %pad_add_fusion.tab_ref, bf16[512,1024]{1,0:T(8,128)(2,1)S(1)} %copy-done.23, bf16[512,512]{1,0:T(8,128)(2,1)} %fusion.4.refs_0_.refs_4_.refs_6_, ...), custom_call_target="tpu_custom_call" | custom-call | flops 4400000000 | tf_op jit(solution)/shard_map/scores/pallas_call | solution.py:126
  88.1 3.8 %all-to-all-start = ((s32[8,1,2]{2,1,0:T(1,128)}), s32[8,1,2]{2,1,0:T(1,128)S(1)}, u32[]{:S(2)}, u32[]{:S(2)}) async-start(s32[8,1,2]{2,1,0:T(1,128)} %copy.15), calls=%async_computation | async-start | bytes 8192 | tf_op jit(solution)/shard_map/all_to_all | solution.py:702
  93.2 7.9 %collective-permute-done.10.refs_2_ = bf16[5,144,128]{2,1,0:T(8,128)(2,1)S(1)} collective-permute-done((bf16[5,144,128]{2,1,0:T(8,128)(2,1)}, bf16[5,144,128]{2,1,0:T(8,128)(2,1)S(1)}, u32[]{:S(2)}, u32[]{:S(2)}) %collective-permute-start.10) | collective-permute-done | bytes 184352 | tf_op jit(solution)/shard_map/ppermute | solution.py:714
  110.0 10.4 %collective-permute-done.13.refs_2_ = bf16[5,144,128]{2,1,0:T(8,128)(2,1)S(1)} collective-permute-done((bf16[5,144,128]{2,1,0:T(8,128)(2,1)S(1)}, bf16[5,144,128]{2,1,0:T(8,128)(2,1)S(1)}, u32[]{:S(2)}, u32[]{:S(2)}) %collective-permute-start.13) | collective-permute-done | bytes 184352 | tf_op jit(solution)/shard_map/ppermute | solution.py:714
  120.5 6.6 %query_gradient.1 = (bf16[256,1024]{1,0:T(8,128)(2,1)S(1)}, bf16[256,1024]{1,0:T(8,128)(2,1)S(1)}, f32[4,128]{1,0:T(4,128)}) custom-call(s32[33]{0:T(128)S(1)} %pad_add_fusion.tab_ref, s32[4,128]{1,0:T(4,128)S(1)} %bitcast.35, bf16[512,1024]{1,0:T(8,128)(2,1)} %copy-done.22, bf16[5,144,128]{2,1,0:T(8,128)(2,1)S(1)} %powers.1.refs_0_, ...), custom_call_target="tpu_custom_call" | custom-call | flops 6600000000 | tf_op jit(solution)/shard_map/query_gradient/pallas_call | solution.py:312
  134.2 8.0 %passage_terms.1 = (bf16[4,128,1024]{2,1,0:T(8,128)(2,1)}, bf16[2,2,128,1024]{3,2,1,0:T(8,128)(2,1)}, bf16[2,2,128,1024]{3,2,1,0:T(8,128)(2,1)}, bf16[2,2,128,10...) custom-call(s32[33]{0:T(128)S(1)} %pad_add_fusion.tab_ref, s32[4,128]{1,0:T(4,128)S(1)} %bitcast.36, ...), custom_call_target="tpu_custom_call" | custom-call | flops 6600000000 | tf_op jit(solution)/shard_map/passage_terms/pallas_call | solution.py:312
  153.6 4.0 %collective-permute-done.21.refs_1_ = bf16[256,1024]{1,0:T(8,128)(2,1)S(1)} collective-permute-done((bf16[256,1024]{1,0:T(8,128)(2,1)S(1)}, bf16[256,1024]{1,0:T(8,128)(2,1)S(1)}, u32[]{:S(2)}, u32[]{:S(2)}) %collective-permute-start.21) | collective-permute-done | bytes 524320 | tf_op jit(solution)/shard_map/ppermute | solution.py:635
  158.6 6.6 %collective-permute-start.23 = (bf16[256,1024]{1,0:T(8,128)(2,1)S(1)}, bf16[256,1024]{1,0:T(8,128)(2,1)S(1)}, u32[]{:S(2)}, u32[]{:S(2)}) collective-permute-start(bf16[256,1024]{1,0:T(8,128)(2,1)S(1)} %get-tuple-element.49.refs_4_), channel_id=1, source_target_pairs={{0,1},{1,0},{2,3},{3,2},{4,5},{5,4},{6,7},{7,6},{8,9},{9,8},{10,11... | collective-permute-start | bytes 1572872 | tf_op jit(solution)/shard_map/ppermute | solution.py:635
  186.4 4.0 %slab_product.2.refs_9_.bottom_ref = bf16[256,1024]{1,0:T(8,128)(2,1)S(1)} custom-call(s32[1]{0:T(128)} %bitcast.tab_ref, f32[256,1024]{1,0:T(8,128)S(1)} %copy-done.58, bf16[256,1024]{1,0:T(8,128)(2,1)} %collective-permute-done.18.refs_0_, bf16[256,1024]{1,0:T(8,128)(2,1)S(1)} %copy-done.42, bf16[256,1024]{1,0:T(8,128)(2,1)S(1)} %copy-done.48, ...), custom_call_target="tpu_custom_call" | custom-call | flops 4400000000 | tf_op jit(solution)/shard_map/slab_product/pallas_call | solution.py:543
  190.4 3.8 %collective-permute-done.16.refs_2_.refs_4_ = bf16[2,2,128,1024]{3,2,1,0:T(8,128)(2,1)S(1)} collective-permute-done((bf16[2,2,128,1024]{3,2,1,0:T(8,128)(2,1)}, bf16[2,2,128,1024]{3,2,1,0:T(8,128)(2,1)S(1)}, u32[]{:S(2)}, u32[]{:S(2)}) %collective-permute-start.16) | collective-permute-done | bytes 1048608 | tf_op jit(solution)/shard_map/ppermute | solution.py:713
  196.7 5.2 %collective-permute-start.25 = (bf16[256,1024]{1,0:T(8,128)(2,1)S(1)}, bf16[256,1024]{1,0:T(8,128)(2,1)S(1)}, u32[]{:S(2)}, u32[]{:S(2)}) collective-permute-start(bf16[256,1024]{1,0:T(8,128)(2,1)S(1)} %get-tuple-element.51.refs_5_), channel_id=1, source_target_pairs={{0,1},{1,0},{2,3},{3,2},{4,5},{5,4},{6,7},{7,6},{8,9},{9,8},{10,11... | collective-permute-start | bytes 1572872 | tf_op jit(solution)/shard_map/ppermute | solution.py:635
  202.0 12.2 %collective-permute-done.25.refs_8_.a_ref = bf16[256,1024]{1,0:T(8,128)(2,1)S(1)} collective-permute-done((bf16[256,1024]{1,0:T(8,128)(2,1)S(1)}, bf16[256,1024]{1,0:T(8,128)(2,1)S(1)}, u32[]{:S(2)}, u32[]{:S(2)}) %collective-permute-start.25) | collective-permute-done | bytes 524320 | tf_op jit(solution)/shard_map/ppermute | solution.py:635
  218.5 3.8 %weight_slabs.6.refs_2_ = bf16[4,512,1024]{2,1,0:T(8,128)(2,1)S(1)} custom-call(s32[4]{0:T(128)S(1)} %pad_add_fusion.4.tab_ref, bf16[512,4096]{1,0:T(8,128)(2,1)S(1)} %copy-done.38, bf16[256,1024]{1,0:T(8,128)(2,1)S(1)} %get-tuple-element.54.top_ref, bf16[256,1024]{1,0:T(8,128)(2,1)S(1)} %get-tuple-element.55.bottom_ref, ...), custom_call_target="tpu_custom_call" | custom-call | flops 4400000000 | tf_op jit(solution)/shard_map/weight_slabs/pallas_call | solution.py:428
  223.1 4.6 %collective-permute-start.33 = (bf16[256,1024]{1,0:T(8,128)(2,1)S(1)}, bf16[256,1024]{1,0:T(8,128)(2,1)S(1)}, u32[]{:S(2)}, u32[]{:S(2)}) collective-permute-start(bf16[256,1024]{1,0:T(8,128)(2,1)S(1)} %get-tuple-element.55.bottom_ref), channel_id=1, source_target_pairs={{0,1},{1,0},{2,3},{3,2},{4,5},{5,4},{6,7},{7,6},{8,9},{9,8},{10,11... | collective-permute-start | bytes 1572872 | tf_op jit(solution)/shard_map/ppermute | solution.py:630
  229.0 11.5 %collective-permute-start.35 = (bf16[256,1024]{1,0:T(8,128)(2,1)S(1)}, bf16[256,1024]{1,0:T(8,128)(2,1)S(1)}, u32[]{:S(2)}, u32[]{:S(2)}) collective-permute-start(bf16[256,1024]{1,0:T(8,128)(2,1)S(1)} %pass_on.9.refs_0_), channel_id=1, source_target_pairs={{0,1},{1,0},{2,3},{3,2},{4,5},{5,4},{6,7},{7,6},{8,9},{9,8},{10,11... | collective-permute-start | bytes 1572872 | tf_op jit(solution)/shard_map/ppermute | solution.py:635
  241.2 4.3 %weight_slabs.7 = (bf16[2,512,512]{2,1,0:T(8,128)(2,1)S(1)}, bf16[2,512,512]{2,1,0:T(8,128)(2,1)S(1)}, bf16[2,512,512]{2,1,0:T(8,128)(2,1)S(1)}, bf16[2,512,512]{2,1,0:T(8,128)(2,1)S(1)}) custom-call(s32[4]{0:T(128)S(1)} %pad_add_fusion.1.tab_ref, bf16[512,4096]{1,0:T(8,128)(2,1)S(1)} %copy-done.38, bf16[256,1024]{1,0:T(8,128)(2,1)S(1)} %get-tuple-element.54.top_ref, ...), custom_call_target="tpu_custom_call" | custom-call | flops 5500000256 | tf_op jit(solution)/shard_map/weight_slabs/pallas_call | solution.py:428
  253.5 6.7 %collective-permute-start.37 = (bf16[256,1024]{1,0:T(8,128)(2,1)S(1)}, bf16[256,1024]{1,0:T(8,128)(2,1)S(1)}, u32[]{:S(2)}, u32[]{:S(2)}) collective-permute-start(bf16[256,1024]{1,0:T(8,128)(2,1)S(1)} %get-tuple-element.64), channel_id=1, source_target_pairs={{0,1},{1,0},{2,3},{3,2},{4,5},{5,4},{6,7},{7,6},{8,9},{9,8},{10,11... | collective-permute-start | bytes 1572872 | tf_op jit(solution)/shard_map/ppermute | solution.py:635
  260.2 10.6 %collective-permute-done.37.refs_1_.refs_2_ = bf16[256,1024]{1,0:T(8,128)(2,1)S(1)} collective-permute-done((bf16[256,1024]{1,0:T(8,128)(2,1)S(1)}, bf16[256,1024]{1,0:T(8,128)(2,1)S(1)}, u32[]{:S(2)}, u32[]{:S(2)}) %collective-permute-start.37) | collective-permute-done | bytes 524320 | tf_op jit(solution)/shard_map/ppermute | solution.py:635
  278.8 4.0 %collective-permute-done.38.a_ref = bf16[256,1024]{1,0:T(8,128)(2,1)S(1)} collective-permute-done((bf16[256,1024]{1,0:T(8,128)(2,1)S(1)}, bf16[256,1024]{1,0:T(8,128)(2,1)S(1)}, u32[]{:S(2)}, u32[]{:S(2)}) %collective-permute-start.38) | collective-permute-done | bytes 524320 | tf_op jit(solution)/shard_map/ppermute | solution.py:635
  (251 shorter events, 123.1 us)
Async XLA Ops:
  13.9 18.2 %collective-permute-start.3 = (bf16[512,512]{1,0:T(8,128)(2,1)}, bf16[512,512]{1,0:T(8,128)(2,1)S(1)}, u32[]{:S(2)}, u32[]{:S(2)}) collective-permute-start(bf16[512,512]{1,0:T(8,128)(2,1)} %fusion.4.refs_0_.refs_4_.refs_6_), channel_id=1, source_target_pairs={{0,16},{4,20},{8,24},{12,28},{16,0},{20,4},{24,8},{28,12},{1,17},{... | collective-permute-start | bytes 1572872 | tf_op jit(solution)/shard_map/ppermute | solution.py:713
  21.5 18.7 %collective-permute-start.4 = (bf16[512,512]{1,0:T(8,128)(2,1)}, bf16[512,512]{1,0:T(8,128)(2,1)S(1)}, u32[]{:S(2)}, u32[]{:S(2)}) collective-permute-start(bf16[512,512]{1,0:T(8,128)(2,1)} %fusion.7.refs_1_.refs_5_.refs_7_), channel_id=1, source_target_pairs={{0,16},{4,20},{8,24},{12,28},{16,0},{20,4},{24,8},{28,12},{1,17},{... | collective-permute-start | bytes 1572872 | tf_op jit(solution)/shard_map/ppermute | solution.py:713
  22.1 19.7 %collective-permute-start.2 = (bf16[512,512]{1,0:T(8,128)(2,1)}, bf16[512,512]{1,0:T(8,128)(2,1)S(1)}, u32[]{:S(2)}, u32[]{:S(2)}) collective-permute-start(bf16[512,512]{1,0:T(8,128)(2,1)} %fusion.7.refs_1_.refs_5_.refs_7_), channel_id=1, source_target_pairs={{0,8},{4,12},{8,0},{12,4},{16,24},{20,28},{24,16},{28,20},{1,9},{5... | collective-permute-start | bytes 1572872 | tf_op jit(solution)/shard_map/ppermute | solution.py:713
  24.4 55.9 %all-to-all-start.1 = ((bf16[4,128,1024]{2,1,0:T(8,128)(2,1)}), bf16[4,128,1024]{2,1,0:T(8,128)(2,1)}, u32[]{:S(2)}, u32[]{:S(2)}) async-start(bf16[4,128,1024]{2,1,0:T(8,128)(2,1)} %dynamic-slice_bitcast_fusion), calls=%async_computation.1 | async-start | bytes 2097152 | tf_op jit(solution)/shard_map/all_to_all | solution.py:718
  29.7 148.9 %all-gather.2.cloned.1.call-start = ((), (), s32[]{:S(2)}) async-start(), calls=%async_computation.2 | async-start | bytes 9437184 | tf_op jit(solution)/shard_map/all_gather | solution.py:745
  32.1 31.6 %collective-permute-start = (bf16[2,512,512]{2,1,0:T(8,128)(2,1)}, bf16[2,512,512]{2,1,0:T(8,128)(2,1)S(1)}, u32[]{:S(2)}, u32[]{:S(2)}) collective-permute-start(bf16[2,512,512]{2,1,0:T(8,128)(2,1)} %stack.88), channel_id=1, source_target_pairs={{0,4},{4,0},{8,12},{12,8},{16,20},{20,16},{24,28},{28,24},{1,5},{5... | collective-permute-start | bytes 3145736 | tf_op jit(solution)/shard_map/ppermute | solution.py:713
  46.4 19.9 %collective-permute-start.5 = (bf16[4,512,512]{2,1,0:T(8,128)(2,1)}, bf16[4,512,512]{2,1,0:T(8,128)(2,1)S(1)}, u32[]{:S(2)}, u32[]{:S(2)}) collective-permute-start(bf16[4,512,512]{2,1,0:T(8,128)(2,1)} %stack.89), channel_id=1, source_target_pairs={{0,4},{4,0},{8,12},{12,8},{16,20},{20,16},{24,28},{28,24},{1,5},{5... | collective-permute-start | bytes 6291464 | tf_op jit(solution)/shard_map/ppermute | solution.py:713
  84.6 16.5 %collective-permute-start.10 = (bf16[5,144,128]{2,1,0:T(8,128)(2,1)}, bf16[5,144,128]{2,1,0:T(8,128)(2,1)S(1)}, u32[]{:S(2)}, u32[]{:S(2)}) collective-permute-start(bf16[5,144,128]{2,1,0:T(8,128)(2,1)} %get-tuple-element.38), channel_id=1, source_target_pairs={{0,2},{1,3},{2,0},{3,1},{4,6},{5,7},{6,4},{7,5},{8,10},{9,11},{10,... | collective-permute-start | bytes 552968 | tf_op jit(solution)/shard_map/ppermute | solution.py:714
  88.1 19.1 %all-to-all-start = ((s32[8,1,2]{2,1,0:T(1,128)}), s32[8,1,2]{2,1,0:T(1,128)S(1)}, u32[]{:S(2)}, u32[]{:S(2)}) async-start(s32[8,1,2]{2,1,0:T(1,128)} %copy.15), calls=%async_computation | async-start | bytes 8192 | tf_op jit(solution)/shard_map/all_to_all | solution.py:702
  104.5 15.9 %collective-permute-start.13 = (bf16[5,144,128]{2,1,0:T(8,128)(2,1)S(1)}, bf16[5,144,128]{2,1,0:T(8,128)(2,1)S(1)}, u32[]{:S(2)}, u32[]{:S(2)}) collective-permute-start(bf16[5,144,128]{2,1,0:T(8,128)(2,1)S(1)} %powers.1.refs_0_), channel_id=1, source_target_pairs={{0,2},{1,3},{2,0},{3,1},{4,6},{5,7},{6,4},{7,5},{8,10},{9,11},{10,... | collective-permute-start | bytes 552968 | tf_op jit(solution)/shard_map/ppermute | solution.py:714
  127.8 17.9 %collective-permute-start.18 = (bf16[256,1024]{1,0:T(8,128)(2,1)S(1)}, bf16[256,1024]{1,0:T(8,128)(2,1)}, u32[]{:S(2)}, u32[]{:S(2)}) collective-permute-start(bf16[256,1024]{1,0:T(8,128)(2,1)S(1)} %get-tuple-element.42.bottom_ref), channel_id=1, source_target_pairs={{0,1},{1,0},{2,3},{3,2},{4,5},{5,4},{6,7},{7,6},{8,9},{9,8},{10,11... | collective-permute-start | bytes 1572872 | tf_op jit(solution)/shard_map/ppermute | solution.py:630
  146.5 43.9 %collective-permute-start.15 = (bf16[2,2,128,1024]{3,2,1,0:T(8,128)(2,1)}, bf16[2,2,128,1024]{3,2,1,0:T(8,128)(2,1)S(1)}, u32[]{:S(2)}, u32[]{:S(2)}) collective-permute-start(bf16[2,2,128,1024]{3,2,1,0:T(8,128)(2,1)} %get-tuple-element.45), channel_id=1, source_target_pairs={{0,8},{4,12},{8,0},{12,4},{16,24},{20,28},{24,16},{28,20},{1,9},{5... | collective-permute-start | bytes 3145736 | tf_op jit(solution)/shard_map/ppermute | solution.py:713
  148.0 46.2 %collective-permute-start.16 = (bf16[2,2,128,1024]{3,2,1,0:T(8,128)(2,1)}, bf16[2,2,128,1024]{3,2,1,0:T(8,128)(2,1)S(1)}, u32[]{:S(2)}, u32[]{:S(2)}) collective-permute-start(bf16[2,2,128,1024]{3,2,1,0:T(8,128)(2,1)} %get-tuple-element.46), channel_id=1, source_target_pairs={{0,16},{4,20},{8,24},{12,28},{16,0},{20,4},{24,8},{28,12},{1,17},{... | collective-permute-start | bytes 3145736 | tf_op jit(solution)/shard_map/ppermute | solution.py:713
  149.6 44.6 %collective-permute-start.17 = (bf16[2,2,128,1024]{3,2,1,0:T(8,128)(2,1)}, bf16[2,2,128,1024]{3,2,1,0:T(8,128)(2,1)}, u32[]{:S(2)}, u32[]{:S(2)}) collective-permute-start(bf16[2,2,128,1024]{3,2,1,0:T(8,128)(2,1)} %get-tuple-element.47), channel_id=1, source_target_pairs={{0,24},{4,28},{8,16},{12,20},{16,8},{20,12},{24,0},{28,4},{1,25},{... | collective-permute-start | bytes 3145736 | tf_op jit(solution)/shard_map/ppermute | solution.py:713
  157.9 18.8 %collective-permute-start.22 = (bf16[256,1024]{1,0:T(8,128)(2,1)S(1)}, bf16[256,1024]{1,0:T(8,128)(2,1)S(1)}, u32[]{:S(2)}, u32[]{:S(2)}) collective-permute-start(bf16[256,1024]{1,0:T(8,128)(2,1)S(1)} %get-tuple-element.50), channel_id=1, source_target_pairs={{1,2},{2,1},{5,6},{6,5},{9,10},{10,9},{13,14},{14,13},{17,18},{18,... | collective-permute-start | bytes 1572872 | tf_op jit(solution)/shard_map/ppermute | solution.py:636
  158.6 18.1 %collective-permute-start.23 = (bf16[256,1024]{1,0:T(8,128)(2,1)S(1)}, bf16[256,1024]{1,0:T(8,128)(2,1)S(1)}, u32[]{:S(2)}, u32[]{:S(2)}) collective-permute-start(bf16[256,1024]{1,0:T(8,128)(2,1)S(1)} %get-tuple-element.49.refs_4_), channel_id=1, source_target_pairs={{0,1},{1,0},{2,3},{3,2},{4,5},{5,4},{6,7},{7,6},{8,9},{9,8},{10,11... | collective-permute-start | bytes 1572872 | tf_op jit(solution)/shard_map/ppermute | solution.py:635
  195.6 18.5 %collective-permute-start.24 = (bf16[4,2,128,1024]{3,2,1,0:T(8,128)(2,1)S(1)}, bf16[4,2,128,1024]{3,2,1,0:T(8,128)(2,1)S(1)}, u32[]{:S(2)}, u32[]{:S(2)}) collective-permute-start(bf16[4,2,128,1024]{3,2,1,0:T(8,128)(2,1)S(1)} %pack.1), channel_id=1, source_target_pairs={{0,4},{4,0},{8,12},{12,8},{16,20},{20,16},{24,28},{28,24},{1,5},{5... | collective-permute-start | bytes 6291464 | tf_op jit(solution)/shard_map/ppermute | solution.py:713
  196.7 17.4 %collective-permute-start.25 = (bf16[256,1024]{1,0:T(8,128)(2,1)S(1)}, bf16[256,1024]{1,0:T(8,128)(2,1)S(1)}, u32[]{:S(2)}, u32[]{:S(2)}) collective-permute-start(bf16[256,1024]{1,0:T(8,128)(2,1)S(1)} %get-tuple-element.51.refs_5_), channel_id=1, source_target_pairs={{0,1},{1,0},{2,3},{3,2},{4,5},{5,4},{6,7},{7,6},{8,9},{9,8},{10,11... | collective-permute-start | bytes 1572872 | tf_op jit(solution)/shard_map/ppermute | solution.py:635
  222.3 18.9 %collective-permute-start.27 = (bf16[4,512,1024]{2,1,0:T(8,128)(2,1)S(1)}, bf16[4,512,1024]{2,1,0:T(8,128)(2,1)S(1)}, u32[]{:S(2)}, u32[]{:S(2)}) collective-permute-start(bf16[4,512,1024]{2,1,0:T(8,128)(2,1)S(1)} %weight_slabs.6.refs_2_), channel_id=1, source_target_pairs={{0,4},{4,0},{8,12},{12,8},{16,20},{20,16},{24,28},{28,24},{1,5},{5... | collective-permute-start | bytes 12582920 | tf_op jit(solution)/shard_map/ppermute | solution.py:713
  223.1 17.5 %collective-permute-start.33 = (bf16[256,1024]{1,0:T(8,128)(2,1)S(1)}, bf16[256,1024]{1,0:T(8,128)(2,1)S(1)}, u32[]{:S(2)}, u32[]{:S(2)}) collective-permute-start(bf16[256,1024]{1,0:T(8,128)(2,1)S(1)} %get-tuple-element.55.bottom_ref), channel_id=1, source_target_pairs={{0,1},{1,0},{2,3},{3,2},{4,5},{5,4},{6,7},{7,6},{8,9},{9,8},{10,11... | collective-permute-start | bytes 1572872 | tf_op jit(solution)/shard_map/ppermute | solution.py:630
  229.0 23.3 %collective-permute-start.35 = (bf16[256,1024]{1,0:T(8,128)(2,1)S(1)}, bf16[256,1024]{1,0:T(8,128)(2,1)S(1)}, u32[]{:S(2)}, u32[]{:S(2)}) collective-permute-start(bf16[256,1024]{1,0:T(8,128)(2,1)S(1)} %pass_on.9.refs_0_), channel_id=1, source_target_pairs={{0,1},{1,0},{2,3},{3,2},{4,5},{5,4},{6,7},{7,6},{8,9},{9,8},{10,11... | collective-permute-start | bytes 1572872 | tf_op jit(solution)/shard_map/ppermute | solution.py:635
  245.6 28.0 %collective-permute-start.28 = (bf16[2,512,512]{2,1,0:T(8,128)(2,1)S(1)}, bf16[2,512,512]{2,1,0:T(8,128)(2,1)S(1)}, u32[]{:S(2)}, u32[]{:S(2)}) collective-permute-start(bf16[2,512,512]{2,1,0:T(8,128)(2,1)S(1)} %get-tuple-element.57), channel_id=1, source_target_pairs={{0,8},{4,12},{8,0},{12,4},{16,24},{20,28},{24,16},{28,20},{1,9},{5... | collective-permute-start | bytes 3145736 | tf_op jit(solution)/shard_map/ppermute | solution.py:713
  246.9 26.7 %collective-permute-start.29 = (bf16[2,512,512]{2,1,0:T(8,128)(2,1)S(1)}, bf16[2,512,512]{2,1,0:T(8,128)(2,1)S(1)}, u32[]{:S(2)}, u32[]{:S(2)}) collective-permute-start(bf16[2,512,512]{2,1,0:T(8,128)(2,1)S(1)} %get-tuple-element.59), channel_id=1, source_target_pairs={{0,16},{4,20},{8,24},{12,28},{16,0},{20,4},{24,8},{28,12},{1,17},{... | collective-permute-start | bytes 3145736 | tf_op jit(solution)/shard_map/ppermute | solution.py:713
  253.5 17.3 %collective-permute-start.37 = (bf16[256,1024]{1,0:T(8,128)(2,1)S(1)}, bf16[256,1024]{1,0:T(8,128)(2,1)S(1)}, u32[]{:S(2)}, u32[]{:S(2)}) collective-permute-start(bf16[256,1024]{1,0:T(8,128)(2,1)S(1)} %get-tuple-element.64), channel_id=1, source_target_pairs={{0,1},{1,0},{2,3},{3,2},{4,5},{5,4},{6,7},{7,6},{8,9},{9,8},{10,11... | collective-permute-start | bytes 1572872 | tf_op jit(solution)/shard_map/ppermute | solution.py:635
  (85 other events, 752.3 us)
Sparse Core Ops, SparseCore 0:
  82.8 55.7 all-gather.1

commit v2 on v1

--- a/solution.py
+++ b/solution.py
@@ -137,7 +137,7 @@
 
 
 def exp_body(slots, rows, tab_ref, pos_ref, *refs):
-    parts, out, ext_ref = refs[:-2], refs[-2], refs[-1]
+    parts, out, ext_ref = refs[:4], refs[-2], refs[-1]
     z = tab_ref[32]
     ext_ref[...] = jnp.zeros_like(ext_ref)
     for i, slot in enumerate(slots[0]):
@@ -161,19 +161,19 @@
         out[i, rows:, :] = ext_ref[...].astype(bf16)
 
 
-def exp_call(slots, rows, tab, pos, parts):
+def exp_call(slots, rows, tab, pos, parts, after):
     shape = parts[0].shape
     return pl.pallas_call(
         functools.partial(exp_body, slots, rows),
         out_shape=jax.ShapeDtypeStruct(shape, bf16),
         grid=(1,),
-        in_specs=[smem_spec(), whole_spec(pos)] + [whole_spec(a) for a in parts],
+        in_specs=[smem_spec(), whole_spec(pos)] + [whole_spec(a) for a in parts] + any_specs(after),
         out_specs=pl.BlockSpec(shape, lambda i: (0, 0, 0)),
         scratch_shapes=[pltpu.VMEM((EXT, rows), f32)],
         compiler_params=params(),
         cost_estimate=cost(1),
         name="powers",
-    )(tab, pos, *parts)
+    )(tab, pos, *parts, *after)
 
 
 def totals_of(mp_count, tab_ref, z, hold, tables, tot, inner, q_sq, e_pos):
@@ -432,7 +432,7 @@
         ),
         out_shape=out_shape,
         compiler_params=params(dimension_semantics=("arbitrary",)),
-        cost_estimate=cost(4 if arrived is None else 5),
+        cost_estimate=cost(1 if earlier is None else 4 if arrived is None else 5),
         name="weight_slabs",
     )(targets, hidden, *d, *more, *after)
 
@@ -553,7 +553,7 @@
         ),
         out_shape=jax.ShapeDtypeStruct(start.shape, bf16),
         compiler_params=params(dimension_semantics=("arbitrary",)),
-        cost_estimate=cost(4),
+        cost_estimate=cost(1),
         name="slab_product",
     )(tab, start, *inner, *outer, weights)
 
@@ -740,14 +740,14 @@
     slots = slots_all(mp_count)
     sent = score_call(tuple(range(dp_count)), slots, rows, tab, eq, sources, ())
     parts = [sent[0]] + [across(sent[k], k) for k in range(1, mp_count)]
-    mine = exp_call(slots, rows, tab, pos, parts)
+    mine = exp_call(slots, rows, tab, pos, parts, (asked,))
     tables = [mine] + [across(mine, k) for k in range(1, mp_count)]
     weights = lax.all_gather(stack([share], (sent[0],))[0], "dp", axis=0)
 
     *dq, loss = back_call(True, mp_count, rows, block_count, tab, pos, eq, tables, sources)
     query_begun = line_start(dq, head_weight, z, mp_count)
     own, here, to_x, to_y, to_d = back_call(
-        False, mp_count, rows, block_count, tab, pos, eq, tables, sources, (query_begun[-1],)
+        False, mp_count, rows, block_count, tab, pos, eq, tables, sources, (dq[0],)
     )
     query_line = line_steps(dq, head_weight, z, mp_count, query_begun, (here,))
     away, home = (7, 3, 5, 1), (6, 2, 4, 0)
@@ -755,7 +755,7 @@
     home_q = weight_slabs(home, me, query_hidden, dq)
     query_bottom = line_bottom(z, mp_count, query_line, weights)
     got = [swap(to_x, 2), swap(to_y, 4), swap(to_d, 6)]
-    other = swap(pack([here] + got, query_line[-1] + [away_q, home_q, asked, query_bottom]), 1)
+    other = swap(pack([here] + got, [query_line[2][-1], query_line[3][-1], away_q, home_q, asked, query_bottom]), 1)
     arrived = {}
     for i, a in enumerate([here] + got):
         arrived[2 * i], arrived[2 * i + 1] = (a, 0), (other, i)
@@ -765,7 +765,7 @@
         asked,
         own,
         [arrived[r] for r in range(dp_count)],
-        [query_line[2][-1], query_line[3][-1]],
+        [],
     )
     passage_begun = line_start(dp, head_weight, z, mp_count)
     away_sum = weight_slabs(away, me, passage_hidden, dp, away_q, None, (passage_begun[-1],))

time: 296 us -> 294 us (level)
  starting transfers between devices: 78.2 us -> 70 us
  blocking collectives: 0 us -> 8.18 us
  waiting for transfers between devices: 76.8 us -> 73 us
  Pallas kernels: 69.7 us -> 73.1 us
    all_to_all x0 -> x1, blocking collectives: none -> 8.18 us  [tables_of(): asked = lax.all_to_all(asks, 'dp', 0, 0, tiled=True).reshape(-1)]
    ppermute x18, waiting for transfers between devices: 23.7 us -> 28.9 us  [neighbours(): swap = lambda a, mask: lax.ppermute(a, 'dp', xor_pairs(dp_count, mask))]
    ppermute x6, waiting for transfers between devices: 31.8 us -> 26.7 us  [line_steps(): inner_swap = lambda a: lax.ppermute(a, 'mp', xor_pairs(mp_count, 1))]
    ppermute x6, waiting for transfers between devices: 21.2 us -> 17.3 us  [neighbours(): across = lambda a, mask: lax.ppermute(a, 'mp', xor_pairs(mp_count, mask))]
    all_to_all x1 -> x0, starting transfers between devices: 3.76 us -> none  [tables_of(): asked = lax.all_to_all(asks, 'dp', 0, 0, tiled=True).reshape(-1)]
    ppermute x6, starting transfers between devices: 32.7 us -> 29.3 us  [line_steps(): inner_swap = lambda a: lax.ppermute(a, 'mp', xor_pairs(mp_count, 1))]
    pallas_call x6, Pallas kernels: 1.48 us -> 4.55 us  [pass_on(): pl.pallas_call(functools.partial(pass_body, [job[3] for job in jobs], len...]
    unnamed x132 -> x128, local copies, waits for them, and re-layouts: 33.5 us -> 32 us
  transfers between devices with their start and end apart: 43 -> 42, of which waited for: 16 -> 16; matrix products, arithmetic and copies ran while one was open for 5% -> 5% of each run, Pallas kernels for 19% -> 21%
where the time goes in v2:
time: 294 us; the launch traced here: 293 us
  Pallas kernels  73.1 us (25%)
  waiting for transfers between devices  73 us (25%)
  starting transfers between devices  70 us (24%)
  local copies, waits for them, and re-layouts  35 us (12%)
  matrix products  16.9 us (6%)
  between operations  14.7 us (5%)
  blocking collectives  8.18 us (3%)
    unnamed x128, local copies, waits for them, and re-layouts  32 us
    ppermute x6, starting transfers between devices, line_steps(): inner_swap = lambda a: lax.ppermute(a, 'mp', xor_pairs(mp_count, 1))  29.3 us
    ppermute x18, waiting for transfers between devices, neighbours(): swap = lambda a, mask: lax.ppermute(a, 'dp', xor_pairs(dp_count, mask))  28.9 us
    ppermute x6, waiting for transfers between devices, line_steps(): inner_swap = lambda a: lax.ppermute(a, 'mp', xor_pairs(mp_count, 1))  26.7 us
    ppermute x6, waiting for transfers between devices, neighbours(): across = lambda a, mask: lax.ppermute(a, 'mp', xor_pairs(mp_count, mask))  17.3 us
    dot_general x3, matrix products, mm(): return lax.dot_general(a, b, dims, preferred_element_type=f32)  16.9 us
    pallas_call x4, Pallas kernels, weight_slabs(): pl.pallas_call(body, grid_spec=pltpu.PrefetchScalarGridSpec(num_scalar_pr...  15.3 us
    ppermute x18, starting transfers between devices, neighbours(): swap = lambda a, mask: lax.ppermute(a, 'dp', xor_pairs(dp_count, mask))  15.2 us
  transfers between devices with their start and end apart: 42, of which 16 were waited for; matrix products, arithmetic and copies ran while one was open for 5% of the time, Pallas kernels for 21%

profile of v2, /device:TPU:0, one launch (start us, length us, event | category | flops | bytes accessed | tf_op | source)
XLA Modules:
  0.0 292.5 jit_solution(16694391207848105174)
XLA Ops:
  7.2 6.7 %fusion.4.refs_0_.refs_4_.refs_6_ = bf16[512,512]{1,0:T(8,128)(2,1)} fusion(bf16[512,4096]{1,0:T(8,128)(2,1)} %hidden_ref.7, bf16[4096,1024]{1,0:T(8,128)(2,1)} %weight_ref.7), kind=kOutput, calls=%fused_computation.5 | convolution fusion | flops 2147745792 | bytes 8912896 | tf_op jit(solution)/shard_map/dot_general | solution.py:22
  24.3 5.4 %all-to-all-start.1 = ((bf16[4,128,1024]{2,1,0:T(8,128)(2,1)}), bf16[4,128,1024]{2,1,0:T(8,128)(2,1)}, u32[]{:S(2)}, u32[]{:S(2)}) async-start(bf16[4,128,1024]{2,1,0:T(8,128)(2,1)} %dynamic-slice_bitcast_fusion), calls=%async_computation.1 | async-start | bytes 2097152 | tf_op jit(solution)/shard_map/all_to_all | solution.py:718
  32.1 8.2 %collective-permute-done.4.refs_3_.refs_9_.refs_15_ = bf16[512,512]{1,0:T(8,128)(2,1)S(1)} collective-permute-done((bf16[512,512]{1,0:T(8,128)(2,1)}, bf16[512,512]{1,0:T(8,128)(2,1)S(1)}, u32[]{:S(2)}, u32[]{:S(2)}) %collective-permute-start.4) | collective-permute-done | bytes 524320 | tf_op jit(solution)/shard_map/ppermute | solution.py:713
  48.4 7.0 %convolution_convert_fusion.refs_2_.eq_ref = bf16[512,1024]{1,0:T(8,128)(2,1)S(1)} fusion(bf16[512,4096]{1,0:T(8,128)(2,1)S(1)} %copy-done.7, bf16[4096,1024]{1,0:T(8,128)(2,1)} %weight_ref.7), kind=kOutput, calls=%fused_computation.4 | convolution fusion | flops 4295491584 | bytes 13631488 | tf_op jit(solution)/shard_map/dot_general | solution.py:22
  55.4 5.5 %collective-permute-done.6.refs_0_.refs_12_.refs_18_ = bf16[512,512]{1,0:T(8,128)(2,1)S(1)} collective-permute-done((bf16[512,512]{1,0:T(8,128)(2,1)}, bf16[512,512]{1,0:T(8,128)(2,1)S(1)}, u32[]{:S(2)}, u32[]{:S(2)}) %collective-permute-start.6) | collective-permute-done | bytes 524320 | tf_op jit(solution)/shard_map/ppermute | solution.py:713
  73.8 5.6 %scores.1 = (bf16[5,144,128]{2,1,0:T(8,128)(2,1)S(1)}, bf16[5,144,128]{2,1,0:T(8,128)(2,1)S(1)}, bf16[5,144,128]{2,1,0:T(8,128)(2,1)S(1)}, bf16[5,144,128]{2,1,0:T(8,128)(2,1)S(1)}) custom-call(s32[33]{0:T(128)S(1)} %pad_add_fusion.tab_ref, bf16[512,1024]{1,0:T(8,128)(2,1)S(1)} %copy-done.26, bf16[512,512]{1,0:T(8,128)(2,1)} %fusion.4.refs_0_.refs_4_.refs_6_, ...), custom_call_target="tpu_custom_call" | custom-call | flops 4400000000 | tf_op jit(solution)/shard_map/scores/pallas_call | solution.py:126
  88.1 8.2 %all_to_all.14 = s32[8,1,2]{2,1,0:T(1,128)S(1)} all-to-all(s32[8,1,2]{2,1,0:T(1,128)S(1)} %copy.15), channel_id=1, replica_groups=mesh['dp'=8,'mp'=4] {'dp'}, dimensions={0} | all-to-all | bytes 128 | tf_op jit(solution)/shard_map/all_to_all | solution.py:702
  97.6 3.9 %collective-permute-done.10.refs_2_ = bf16[5,144,128]{2,1,0:T(8,128)(2,1)S(1)} collective-permute-done((bf16[5,144,128]{2,1,0:T(8,128)(2,1)S(1)}, bf16[5,144,128]{2,1,0:T(8,128)(2,1)S(1)}, u32[]{:S(2)}, u32[]{:S(2)}) %collective-permute-start.10) | collective-permute-done | bytes 184352 | tf_op jit(solution)/shard_map/ppermute | solution.py:714
  110.4 10.4 %collective-permute-done.13.refs_2_ = bf16[5,144,128]{2,1,0:T(8,128)(2,1)S(1)} collective-permute-done((bf16[5,144,128]{2,1,0:T(8,128)(2,1)S(1)}, bf16[5,144,128]{2,1,0:T(8,128)(2,1)S(1)}, u32[]{:S(2)}, u32[]{:S(2)}) %collective-permute-start.13) | collective-permute-done | bytes 184352 | tf_op jit(solution)/shard_map/ppermute | solution.py:714
  120.8 7.1 %query_gradient.1 = (bf16[256,1024]{1,0:T(8,128)(2,1)S(1)}, bf16[256,1024]{1,0:T(8,128)(2,1)S(1)}, f32[4,128]{1,0:T(4,128)}) custom-call(s32[33]{0:T(128)S(1)} %pad_add_fusion.tab_ref, s32[4,128]{1,0:T(4,128)S(1)} %bitcast.35, bf16[512,1024]{1,0:T(8,128)(2,1)} %copy-done.25, bf16[5,144,128]{2,1,0:T(8,128)(2,1)S(1)} %powers.1.refs_0_, ...), custom_call_target="tpu_custom_call" | custom-call | flops 6600000000 | tf_op jit(solution)/shard_map/query_gradient/pallas_call | solution.py:312
  132.8 7.4 %passage_terms.1 = (bf16[4,128,1024]{2,1,0:T(8,128)(2,1)}, bf16[2,2,128,1024]{3,2,1,0:T(8,128)(2,1)}, bf16[2,2,128,1024]{3,2,1,0:T(8,128)(2,1)}, bf16[2,2,128,10...) custom-call(s32[33]{0:T(128)S(1)} %pad_add_fusion.tab_ref, s32[4,128]{1,0:T(4,128)S(1)} %bitcast.36, ...), custom_call_target="tpu_custom_call" | custom-call | flops 6600000000 | tf_op jit(solution)/shard_map/passage_terms/pallas_call | solution.py:312
  148.1 6.2 %collective-permute-done.21.refs_1_ = bf16[256,1024]{1,0:T(8,128)(2,1)S(1)} collective-permute-done((bf16[256,1024]{1,0:T(8,128)(2,1)S(1)}, bf16[256,1024]{1,0:T(8,128)(2,1)S(1)}, u32[]{:S(2)}, u32[]{:S(2)}) %collective-permute-start.21) | collective-permute-done | bytes 524320 | tf_op jit(solution)/shard_map/ppermute | solution.py:635
  157.0 5.9 %collective-permute-start.23 = (bf16[256,1024]{1,0:T(8,128)(2,1)}, bf16[256,1024]{1,0:T(8,128)(2,1)}, u32[]{:S(2)}, u32[]{:S(2)}) collective-permute-start(bf16[256,1024]{1,0:T(8,128)(2,1)} %get-tuple-element.50), channel_id=1, source_target_pairs={{0,1},{1,0},{2,3},{3,2},{4,5},{5,4},{6,7},{7,6},{8,9},{9,8},{10,11... | collective-permute-start | bytes 1572872 | tf_op jit(solution)/shard_map/ppermute | solution.py:635
  166.4 6.0 %collective-permute-done.23.refs_1_.refs_2_ = bf16[256,1024]{1,0:T(8,128)(2,1)} collective-permute-done((bf16[256,1024]{1,0:T(8,128)(2,1)}, bf16[256,1024]{1,0:T(8,128)(2,1)}, u32[]{:S(2)}, u32[]{:S(2)}) %collective-permute-start.23) | collective-permute-done | bytes 524320 | tf_op jit(solution)/shard_map/ppermute | solution.py:635
  180.6 3.7 %weight_slabs.5.refs_7_.earlier_ref = bf16[4,512,1024]{2,1,0:T(8,128)(2,1)S(1)} custom-call(s32[4]{0:T(128)S(1)} %pad_add_fusion.2.tab_ref, bf16[512,4096]{1,0:T(8,128)(2,1)S(1)} %copy-done.8, bf16[256,1024]{1,0:T(8,128)(2,1)S(1)} %copy-done.10, bf16[256,1024]{1,0:T(8,128)(2,1)S(1)} %get-tuple-element.47.bottom_ref), custom_call_target="tpu_custom_call" | custom-call | flops 1100000000 | tf_op jit(solution)/shard_map/weight_slabs/pallas_call | solution.py:428
  186.2 3.7 %weight_slabs.4.refs_6_.refs_0_ = bf16[4,512,1024]{2,1,0:T(8,128)(2,1)S(1)} custom-call(s32[4]{0:T(128)S(1)} %pad_add_fusion.4.tab_ref, bf16[512,4096]{1,0:T(8,128)(2,1)S(1)} %copy-done.8, bf16[256,1024]{1,0:T(8,128)(2,1)S(1)} %copy-done.10, bf16[256,1024]{1,0:T(8,128)(2,1)S(1)} %get-tuple-element.47.bottom_ref), custom_call_target="tpu_custom_call" | custom-call | flops 1100000000 | tf_op jit(solution)/shard_map/weight_slabs/pallas_call | solution.py:428
  199.8 4.1 %slab_product.2.refs_9_.bottom_ref = bf16[256,1024]{1,0:T(8,128)(2,1)S(1)} custom-call(s32[1]{0:T(128)} %bitcast.tab_ref, f32[256,1024]{1,0:T(8,128)S(1)} %copy-done.28, bf16[256,1024]{1,0:T(8,128)(2,1)} %collective-permute-done.18.refs_0_, bf16[256,1024]{1,0:T(8,128)(2,1)S(1)} %copy-done.37, bf16[256,1024]{1,0:T(8,128)(2,1)} %collective-permute-done.23.refs_1_.refs_2_, ...), custom_call_target="tpu_custom_call" | custom-call | flops 1100000000 | tf_op jit(solution)/shard_map/slab_product/pallas_call | solution.py:543
  203.9 4.9 %collective-permute-done.16.refs_2_.refs_4_ = bf16[2,2,128,1024]{3,2,1,0:T(8,128)(2,1)} collective-permute-done((bf16[2,2,128,1024]{3,2,1,0:T(8,128)(2,1)}, bf16[2,2,128,1024]{3,2,1,0:T(8,128)(2,1)}, u32[]{:S(2)}, u32[]{:S(2)}) %collective-permute-start.16) | collective-permute-done | bytes 1048608 | tf_op jit(solution)/shard_map/ppermute | solution.py:713
  210.3 4.1 %collective-permute-done.26.refs_1_.refs_3_.refs_5_.refs_7_ = bf16[4,2,128,1024]{3,2,1,0:T(8,128)(2,1)S(1)} collective-permute-done((bf16[4,2,128,1024]{3,2,1,0:T(8,128)(2,1)S(1)}, bf16[4,2,128,1024]{3,2,1,0:T(8,128)(2,1)S(1)}, u32[]{:S(2)}, u32[]{:S(2)}) %collective-permute-start.26) | collective-permute-done | bytes 2097184 | tf_op jit(solution)/shard_map/ppermute | solution.py:713
  219.0 3.7 %weight_slabs.6.refs_2_ = bf16[4,512,1024]{2,1,0:T(8,128)(2,1)S(1)} custom-call(s32[4]{0:T(128)S(1)} %pad_add_fusion.4.tab_ref, bf16[512,4096]{1,0:T(8,128)(2,1)S(1)} %copy-done.43, bf16[256,1024]{1,0:T(8,128)(2,1)S(1)} %get-tuple-element.54.top_ref, bf16[256,1024]{1,0:T(8,128)(2,1)S(1)} %get-tuple-element.55.bottom_ref, ...), custom_call_target="tpu_custom_call" | custom-call | flops 4400000000 | tf_op jit(solution)/shard_map/weight_slabs/pallas_call | solution.py:428
  228.1 11.5 %collective-permute-start.35 = (bf16[256,1024]{1,0:T(8,128)(2,1)S(1)}, bf16[256,1024]{1,0:T(8,128)(2,1)S(1)}, u32[]{:S(2)}, u32[]{:S(2)}) collective-permute-start(bf16[256,1024]{1,0:T(8,128)(2,1)S(1)} %pass_on.9.refs_0_), channel_id=1, source_target_pairs={{0,1},{1,0},{2,3},{3,2},{4,5},{5,4},{6,7},{7,6},{8,9},{9,8},{10,11... | collective-permute-start | bytes 1572872 | tf_op jit(solution)/shard_map/ppermute | solution.py:635
  240.2 4.2 %weight_slabs.7 = (bf16[2,512,512]{2,1,0:T(8,128)(2,1)S(1)}, bf16[2,512,512]{2,1,0:T(8,128)(2,1)S(1)}, bf16[2,512,512]{2,1,0:T(8,128)(2,1)S(1)}, bf16[2,512,512]{2,1,0:T(8,128)(2,1)S(1)}) custom-call(s32[4]{0:T(128)S(1)} %pad_add_fusion.2.tab_ref, bf16[512,4096]{1,0:T(8,128)(2,1)S(1)} %copy-done.43, bf16[256,1024]{1,0:T(8,128)(2,1)S(1)} %get-tuple-element.54.top_ref, ...), custom_call_target="tpu_custom_call" | custom-call | flops 5500000256 | tf_op jit(solution)/shard_map/weight_slabs/pallas_call | solution.py:428
  252.4 6.3 %collective-permute-start.37 = (bf16[256,1024]{1,0:T(8,128)(2,1)S(1)}, bf16[256,1024]{1,0:T(8,128)(2,1)S(1)}, u32[]{:S(2)}, u32[]{:S(2)}) collective-permute-start(bf16[256,1024]{1,0:T(8,128)(2,1)S(1)} %get-tuple-element.64), channel_id=1, source_target_pairs={{0,1},{1,0},{2,3},{3,2},{4,5},{5,4},{6,7},{7,6},{8,9},{9,8},{10,11... | collective-permute-start | bytes 1572872 | tf_op jit(solution)/shard_map/ppermute | solution.py:635
  258.7 10.1 %collective-permute-done.37.refs_1_.refs_2_ = bf16[256,1024]{1,0:T(8,128)(2,1)S(1)} collective-permute-done((bf16[256,1024]{1,0:T(8,128)(2,1)S(1)}, bf16[256,1024]{1,0:T(8,128)(2,1)S(1)}, u32[]{:S(2)}, u32[]{:S(2)}) %collective-permute-start.37) | collective-permute-done | bytes 524320 | tf_op jit(solution)/shard_map/ppermute | solution.py:635
  (246 shorter events, 127.9 us)
Async XLA Ops:
  13.9 18.2 %collective-permute-start.3 = (bf16[512,512]{1,0:T(8,128)(2,1)}, bf16[512,512]{1,0:T(8,128)(2,1)S(1)}, u32[]{:S(2)}, u32[]{:S(2)}) collective-permute-start(bf16[512,512]{1,0:T(8,128)(2,1)} %fusion.4.refs_0_.refs_4_.refs_6_), channel_id=1, source_target_pairs={{0,16},{4,20},{8,24},{12,28},{16,0},{20,4},{24,8},{28,12},{1,17},{... | collective-permute-start | bytes 1572872 | tf_op jit(solution)/shard_map/ppermute | solution.py:713
  16.9 15.2 %collective-permute-start.1 = (bf16[512,512]{1,0:T(8,128)(2,1)}, bf16[512,512]{1,0:T(8,128)(2,1)S(1)}, u32[]{:S(2)}, u32[]{:S(2)}) collective-permute-start(bf16[512,512]{1,0:T(8,128)(2,1)} %fusion.4.refs_0_.refs_4_.refs_6_), channel_id=1, source_target_pairs={{0,8},{4,12},{8,0},{12,4},{16,24},{20,28},{24,16},{28,20},{1,9},{5... | collective-permute-start | bytes 1572872 | tf_op jit(solution)/shard_map/ppermute | solution.py:713
  21.5 18.7 %collective-permute-start.4 = (bf16[512,512]{1,0:T(8,128)(2,1)}, bf16[512,512]{1,0:T(8,128)(2,1)S(1)}, u32[]{:S(2)}, u32[]{:S(2)}) collective-permute-start(bf16[512,512]{1,0:T(8,128)(2,1)} %fusion.7.refs_1_.refs_5_.refs_7_), channel_id=1, source_target_pairs={{0,16},{4,20},{8,24},{12,28},{16,0},{20,4},{24,8},{28,12},{1,17},{... | collective-permute-start | bytes 1572872 | tf_op jit(solution)/shard_map/ppermute | solution.py:713
  22.0 19.7 %collective-permute-start.2 = (bf16[512,512]{1,0:T(8,128)(2,1)}, bf16[512,512]{1,0:T(8,128)(2,1)S(1)}, u32[]{:S(2)}, u32[]{:S(2)}) collective-permute-start(bf16[512,512]{1,0:T(8,128)(2,1)} %fusion.7.refs_1_.refs_5_.refs_7_), channel_id=1, source_target_pairs={{0,8},{4,12},{8,0},{12,4},{16,24},{20,28},{24,16},{28,20},{1,9},{5... | collective-permute-start | bytes 1572872 | tf_op jit(solution)/shard_map/ppermute | solution.py:713
  24.3 56.5 %all-to-all-start.1 = ((bf16[4,128,1024]{2,1,0:T(8,128)(2,1)}), bf16[4,128,1024]{2,1,0:T(8,128)(2,1)}, u32[]{:S(2)}, u32[]{:S(2)}) async-start(bf16[4,128,1024]{2,1,0:T(8,128)(2,1)} %dynamic-slice_bitcast_fusion), calls=%async_computation.1 | async-start | bytes 2097152 | tf_op jit(solution)/shard_map/all_to_all | solution.py:718
  29.7 162.3 %all-gather.2.cloned.1.call-start = ((), (), s32[]{:S(2)}) async-start(), calls=%async_computation.2 | async-start | bytes 9437184 | tf_op jit(solution)/shard_map/all_gather | solution.py:745
  32.1 31.7 %collective-permute-start = (bf16[2,512,512]{2,1,0:T(8,128)(2,1)}, bf16[2,512,512]{2,1,0:T(8,128)(2,1)S(1)}, u32[]{:S(2)}, u32[]{:S(2)}) collective-permute-start(bf16[2,512,512]{2,1,0:T(8,128)(2,1)} %stack.85), channel_id=1, source_target_pairs={{0,4},{4,0},{8,12},{12,8},{16,20},{20,16},{24,28},{28,24},{1,5},{5... | collective-permute-start | bytes 3145736 | tf_op jit(solution)/shard_map/ppermute | solution.py:713
  46.4 19.9 %collective-permute-start.5 = (bf16[4,512,512]{2,1,0:T(8,128)(2,1)}, bf16[4,512,512]{2,1,0:T(8,128)(2,1)S(1)}, u32[]{:S(2)}, u32[]{:S(2)}) collective-permute-start(bf16[4,512,512]{2,1,0:T(8,128)(2,1)} %stack.86), channel_id=1, source_target_pairs={{0,4},{4,0},{8,12},{12,8},{16,20},{20,16},{24,28},{28,24},{1,5},{5... | collective-permute-start | bytes 6291464 | tf_op jit(solution)/shard_map/ppermute | solution.py:713
  46.4 14.5 %collective-permute-start.6 = (bf16[512,512]{1,0:T(8,128)(2,1)}, bf16[512,512]{1,0:T(8,128)(2,1)S(1)}, u32[]{:S(2)}, u32[]{:S(2)}) collective-permute-start(bf16[512,512]{1,0:T(8,128)(2,1)} %copy-done.16), channel_id=1, source_target_pairs={{0,16},{4,20},{8,24},{12,28},{16,0},{20,4},{24,8},{28,12},{1,17},{... | collective-permute-start | bytes 1572872 | tf_op jit(solution)/shard_map/ppermute | solution.py:713
  46.7 14.3 %collective-permute-start.7 = (bf16[512,512]{1,0:T(8,128)(2,1)}, bf16[512,512]{1,0:T(8,128)(2,1)S(1)}, u32[]{:S(2)}, u32[]{:S(2)}) collective-permute-start(bf16[512,512]{1,0:T(8,128)(2,1)} %copy-done.19), channel_id=1, source_target_pairs={{0,8},{4,12},{8,0},{12,4},{16,24},{20,28},{24,16},{28,20},{1,9},{5... | collective-permute-start | bytes 1572872 | tf_op jit(solution)/shard_map/ppermute | solution.py:713
  85.2 16.3 %collective-permute-start.10 = (bf16[5,144,128]{2,1,0:T(8,128)(2,1)S(1)}, bf16[5,144,128]{2,1,0:T(8,128)(2,1)S(1)}, u32[]{:S(2)}, u32[]{:S(2)}) collective-permute-start(bf16[5,144,128]{2,1,0:T(8,128)(2,1)S(1)} %copy-done.45), channel_id=1, source_target_pairs={{0,2},{1,3},{2,0},{3,1},{4,6},{5,7},{6,4},{7,5},{8,10},{9,11},{10,... | collective-permute-start | bytes 552968 | tf_op jit(solution)/shard_map/ppermute | solution.py:714
  104.9 15.9 %collective-permute-start.13 = (bf16[5,144,128]{2,1,0:T(8,128)(2,1)S(1)}, bf16[5,144,128]{2,1,0:T(8,128)(2,1)S(1)}, u32[]{:S(2)}, u32[]{:S(2)}) collective-permute-start(bf16[5,144,128]{2,1,0:T(8,128)(2,1)S(1)} %powers.1.refs_0_), channel_id=1, source_target_pairs={{0,2},{1,3},{2,0},{3,1},{4,6},{5,7},{6,4},{7,5},{8,10},{9,11},{10,... | collective-permute-start | bytes 552968 | tf_op jit(solution)/shard_map/ppermute | solution.py:714
  157.0 15.5 %collective-permute-start.23 = (bf16[256,1024]{1,0:T(8,128)(2,1)}, bf16[256,1024]{1,0:T(8,128)(2,1)}, u32[]{:S(2)}, u32[]{:S(2)}) collective-permute-start(bf16[256,1024]{1,0:T(8,128)(2,1)} %get-tuple-element.50), channel_id=1, source_target_pairs={{0,1},{1,0},{2,3},{3,2},{4,5},{5,4},{6,7},{7,6},{8,9},{9,8},{10,11... | collective-permute-start | bytes 1572872 | tf_op jit(solution)/shard_map/ppermute | solution.py:635
  162.9 41.0 %collective-permute-start.15 = (bf16[2,2,128,1024]{3,2,1,0:T(8,128)(2,1)}, bf16[2,2,128,1024]{3,2,1,0:T(8,128)(2,1)S(1)}, u32[]{:S(2)}, u32[]{:S(2)}) collective-permute-start(bf16[2,2,128,1024]{3,2,1,0:T(8,128)(2,1)} %get-tuple-element.44), channel_id=1, source_target_pairs={{0,8},{4,12},{8,0},{12,4},{16,24},{20,28},{24,16},{28,20},{1,9},{5... | collective-permute-start | bytes 3145736 | tf_op jit(solution)/shard_map/ppermute | solution.py:713
  164.4 44.4 %collective-permute-start.16 = (bf16[2,2,128,1024]{3,2,1,0:T(8,128)(2,1)}, bf16[2,2,128,1024]{3,2,1,0:T(8,128)(2,1)}, u32[]{:S(2)}, u32[]{:S(2)}) collective-permute-start(bf16[2,2,128,1024]{3,2,1,0:T(8,128)(2,1)} %get-tuple-element.45), channel_id=1, source_target_pairs={{0,16},{4,20},{8,24},{12,28},{16,0},{20,4},{24,8},{28,12},{1,17},{... | collective-permute-start | bytes 3145736 | tf_op jit(solution)/shard_map/ppermute | solution.py:713
  165.9 42.9 %collective-permute-start.17 = (bf16[2,2,128,1024]{3,2,1,0:T(8,128)(2,1)}, bf16[2,2,128,1024]{3,2,1,0:T(8,128)(2,1)}, u32[]{:S(2)}, u32[]{:S(2)}) collective-permute-start(bf16[2,2,128,1024]{3,2,1,0:T(8,128)(2,1)} %get-tuple-element.46), channel_id=1, source_target_pairs={{0,24},{4,28},{8,16},{12,20},{16,8},{20,12},{24,0},{28,4},{1,25},{... | collective-permute-start | bytes 3145736 | tf_op jit(solution)/shard_map/ppermute | solution.py:713
  177.2 31.7 %collective-permute-start.24 = (bf16[256,1024]{1,0:T(8,128)(2,1)}, bf16[256,1024]{1,0:T(8,128)(2,1)}, u32[]{:S(2)}, u32[]{:S(2)}) collective-permute-start(bf16[256,1024]{1,0:T(8,128)(2,1)} %get-tuple-element.51), channel_id=1, source_target_pairs={{0,1},{1,0},{2,3},{3,2},{4,5},{5,4},{6,7},{7,6},{8,9},{9,8},{10,11... | collective-permute-start | bytes 1572872 | tf_op jit(solution)/shard_map/ppermute | solution.py:635
  179.0 29.9 %collective-permute-start.25 = (bf16[256,1024]{1,0:T(8,128)(2,1)}, bf16[256,1024]{1,0:T(8,128)(2,1)}, u32[]{:S(2)}, u32[]{:S(2)}) collective-permute-start(bf16[256,1024]{1,0:T(8,128)(2,1)} %get-tuple-element.52), channel_id=1, source_target_pairs={{1,2},{2,1},{5,6},{6,5},{9,10},{10,9},{13,14},{14,13},{17,18},{18,... | collective-permute-start | bytes 1572872 | tf_op jit(solution)/shard_map/ppermute | solution.py:636
  222.7 17.5 %collective-permute-start.27 = (bf16[4,512,1024]{2,1,0:T(8,128)(2,1)S(1)}, bf16[4,512,1024]{2,1,0:T(8,128)(2,1)S(1)}, u32[]{:S(2)}, u32[]{:S(2)}) collective-permute-start(bf16[4,512,1024]{2,1,0:T(8,128)(2,1)S(1)} %weight_slabs.6.refs_2_), channel_id=1, source_target_pairs={{0,4},{4,0},{8,12},{12,8},{16,20},{20,16},{24,28},{28,24},{1,5},{5... | collective-permute-start | bytes 12582920 | tf_op jit(solution)/shard_map/ppermute | solution.py:713
  223.6 15.9 %collective-permute-start.33 = (bf16[256,1024]{1,0:T(8,128)(2,1)S(1)}, bf16[256,1024]{1,0:T(8,128)(2,1)S(1)}, u32[]{:S(2)}, u32[]{:S(2)}) collective-permute-start(bf16[256,1024]{1,0:T(8,128)(2,1)S(1)} %get-tuple-element.55.bottom_ref), channel_id=1, source_target_pairs={{0,1},{1,0},{2,3},{3,2},{4,5},{5,4},{6,7},{7,6},{8,9},{9,8},{10,11... | collective-permute-start | bytes 1572872 | tf_op jit(solution)/shard_map/ppermute | solution.py:630
  228.1 23.1 %collective-permute-start.35 = (bf16[256,1024]{1,0:T(8,128)(2,1)S(1)}, bf16[256,1024]{1,0:T(8,128)(2,1)S(1)}, u32[]{:S(2)}, u32[]{:S(2)}) collective-permute-start(bf16[256,1024]{1,0:T(8,128)(2,1)S(1)} %pass_on.9.refs_0_), channel_id=1, source_target_pairs={{0,1},{1,0},{2,3},{3,2},{4,5},{5,4},{6,7},{7,6},{8,9},{9,8},{10,11... | collective-permute-start | bytes 1572872 | tf_op jit(solution)/shard_map/ppermute | solution.py:635
  244.5 27.1 %collective-permute-start.28 = (bf16[2,512,512]{2,1,0:T(8,128)(2,1)S(1)}, bf16[2,512,512]{2,1,0:T(8,128)(2,1)S(1)}, u32[]{:S(2)}, u32[]{:S(2)}) collective-permute-start(bf16[2,512,512]{2,1,0:T(8,128)(2,1)S(1)} %get-tuple-element.57), channel_id=1, source_target_pairs={{0,8},{4,12},{8,0},{12,4},{16,24},{20,28},{24,16},{28,20},{1,9},{5... | collective-permute-start | bytes 3145736 | tf_op jit(solution)/shard_map/ppermute | solution.py:713
  245.7 26.0 %collective-permute-start.29 = (bf16[2,512,512]{2,1,0:T(8,128)(2,1)S(1)}, bf16[2,512,512]{2,1,0:T(8,128)(2,1)S(1)}, u32[]{:S(2)}, u32[]{:S(2)}) collective-permute-start(bf16[2,512,512]{2,1,0:T(8,128)(2,1)S(1)} %get-tuple-element.59), channel_id=1, source_target_pairs={{0,16},{4,20},{8,24},{12,28},{16,0},{20,4},{24,8},{28,12},{1,17},{... | collective-permute-start | bytes 3145736 | tf_op jit(solution)/shard_map/ppermute | solution.py:713
  252.4 16.5 %collective-permute-start.37 = (bf16[256,1024]{1,0:T(8,128)(2,1)S(1)}, bf16[256,1024]{1,0:T(8,128)(2,1)S(1)}, u32[]{:S(2)}, u32[]{:S(2)}) collective-permute-start(bf16[256,1024]{1,0:T(8,128)(2,1)S(1)} %get-tuple-element.64), channel_id=1, source_target_pairs={{0,1},{1,0},{2,3},{3,2},{4,5},{5,4},{6,7},{7,6},{8,9},{9,8},{10,11... | collective-permute-start | bytes 1572872 | tf_op jit(solution)/shard_map/ppermute | solution.py:635
  (82 other events, 703.5 us)
Sparse Core Ops, SparseCore 0:
  83.4 55.6 all-gather.1

commit v3 on v2

--- a/solution.py
+++ b/solution.py
@@ -222,7 +222,7 @@
             refs[4][...] = jnp.zeros_like(refs[4])
             positive = jnp.log(e_pos[...])
             loss_out[...] = jnp.log(tot[...]) - positive
-            inner[...] = inner[...] / tot[...] - positive
+            inner[...] = (inner[...] - positive * tot[...]) / tot[...]
 
     def visit(place, sources, at, qb, is_own, out_ref=None):
         owner, i = place
@@ -233,7 +233,7 @@
         weight = powers * (1.0 / total)
         if is_own:
             match = lax.broadcasted_iota(jnp.int32, (rows, rows), 0) == pos_ref[pl.ds(qb, 1), :]
-            weight = jnp.where(match, e_pos[pl.ds(qb, 1), :] / total - 1.0, weight)
+            weight = jnp.where(match, (e_pos[pl.ds(qb, 1), :] - total) / total, weight)
         to_q = weight * (p_inv * (1.0 / logit_divisor))
         rows_of_q = pl.ds(qb * rows, rows)
         if to_query:

time: 294 us -> 294 us (level)
  no operation moved by 1% of the time
where the time goes in v3:
time: 294 us; the launch traced here: 292 us
  waiting for transfers between devices  73.2 us (25%)
  Pallas kernels  73.1 us (25%)
  starting transfers between devices  69.9 us (24%)
  local copies, waits for them, and re-layouts  35 us (12%)
  matrix products  16.9 us (6%)
  between operations  14.7 us (5%)
  blocking collectives  8.18 us (3%)
    unnamed x128, local copies, waits for them, and re-layouts  32 us
    ppermute x6, starting transfers between devices, line_steps(): inner_swap = lambda a: lax.ppermute(a, 'mp', xor_pairs(mp_count, 1))  29.2 us
    ppermute x18, waiting for transfers between devices, neighbours(): swap = lambda a, mask: lax.ppermute(a, 'dp', xor_pairs(dp_count, mask))  29 us
    ppermute x6, waiting for transfers between devices, line_steps(): inner_swap = lambda a: lax.ppermute(a, 'mp', xor_pairs(mp_count, 1))  26.8 us
    ppermute x6, waiting for transfers between devices, neighbours(): across = lambda a, mask: lax.ppermute(a, 'mp', xor_pairs(mp_count, mask))  17.3 us
    dot_general x3, matrix products, mm(): return lax.dot_general(a, b, dims, preferred_element_type=f32)  16.9 us
    pallas_call x4, Pallas kernels, weight_slabs(): pl.pallas_call(body, grid_spec=pltpu.PrefetchScalarGridSpec(num_scalar_pr...  15.3 us
    ppermute x18, starting transfers between devices, neighbours(): swap = lambda a, mask: lax.ppermute(a, 'dp', xor_pairs(dp_count, mask))  15.1 us
  transfers between devices with their start and end apart: 42, of which 16 were waited for; matrix products, arithmetic and copies ran while one was open for 5% of the time, Pallas kernels for 21%

profile of v3, /device:TPU:0, one launch (start us, length us, event | category | flops | bytes accessed | tf_op | source)
XLA Modules:
  0.0 292.5 jit_solution(1749526686926304059)
XLA Ops:
  7.2 6.7 %fusion.4.refs_0_.refs_4_.refs_6_ = bf16[512,512]{1,0:T(8,128)(2,1)} fusion(bf16[512,4096]{1,0:T(8,128)(2,1)} %hidden_ref.7, bf16[4096,1024]{1,0:T(8,128)(2,1)} %weight_ref.7), kind=kOutput, calls=%fused_computation.5 | convolution fusion | flops 2147745792 | bytes 8912896 | tf_op jit(solution)/shard_map/dot_general | solution.py:22
  24.3 5.4 %all-to-all-start.1 = ((bf16[4,128,1024]{2,1,0:T(8,128)(2,1)}), bf16[4,128,1024]{2,1,0:T(8,128)(2,1)}, u32[]{:S(2)}, u32[]{:S(2)}) async-start(bf16[4,128,1024]{2,1,0:T(8,128)(2,1)} %dynamic-slice_bitcast_fusion), calls=%async_computation.1 | async-start | bytes 2097152 | tf_op jit(solution)/shard_map/all_to_all | solution.py:718
  32.1 8.2 %collective-permute-done.4.refs_3_.refs_9_.refs_15_ = bf16[512,512]{1,0:T(8,128)(2,1)S(1)} collective-permute-done((bf16[512,512]{1,0:T(8,128)(2,1)}, bf16[512,512]{1,0:T(8,128)(2,1)S(1)}, u32[]{:S(2)}, u32[]{:S(2)}) %collective-permute-start.4) | collective-permute-done | bytes 524320 | tf_op jit(solution)/shard_map/ppermute | solution.py:713
  48.4 7.0 %convolution_convert_fusion.refs_2_.eq_ref = bf16[512,1024]{1,0:T(8,128)(2,1)S(1)} fusion(bf16[512,4096]{1,0:T(8,128)(2,1)S(1)} %copy-done.7, bf16[4096,1024]{1,0:T(8,128)(2,1)} %weight_ref.7), kind=kOutput, calls=%fused_computation.4 | convolution fusion | flops 4295491584 | bytes 13631488 | tf_op jit(solution)/shard_map/dot_general | solution.py:22
  55.4 5.5 %collective-permute-done.6.refs_0_.refs_12_.refs_18_ = bf16[512,512]{1,0:T(8,128)(2,1)S(1)} collective-permute-done((bf16[512,512]{1,0:T(8,128)(2,1)}, bf16[512,512]{1,0:T(8,128)(2,1)S(1)}, u32[]{:S(2)}, u32[]{:S(2)}) %collective-permute-start.6) | collective-permute-done | bytes 524320 | tf_op jit(solution)/shard_map/ppermute | solution.py:713
  73.8 5.6 %scores.1 = (bf16[5,144,128]{2,1,0:T(8,128)(2,1)S(1)}, bf16[5,144,128]{2,1,0:T(8,128)(2,1)S(1)}, bf16[5,144,128]{2,1,0:T(8,128)(2,1)S(1)}, bf16[5,144,128]{2,1,0:T(8,128)(2,1)S(1)}) custom-call(s32[33]{0:T(128)S(1)} %pad_add_fusion.tab_ref, bf16[512,1024]{1,0:T(8,128)(2,1)S(1)} %copy-done.26, bf16[512,512]{1,0:T(8,128)(2,1)} %fusion.4.refs_0_.refs_4_.refs_6_, ...), custom_call_target="tpu_custom_call" | custom-call | flops 4400000000 | tf_op jit(solution)/shard_map/scores/pallas_call | solution.py:126
  88.1 8.2 %all_to_all.14 = s32[8,1,2]{2,1,0:T(1,128)S(1)} all-to-all(s32[8,1,2]{2,1,0:T(1,128)S(1)} %copy.15), channel_id=1, replica_groups=mesh['dp'=8,'mp'=4] {'dp'}, dimensions={0} | all-to-all | bytes 128 | tf_op jit(solution)/shard_map/all_to_all | solution.py:702
  97.6 3.9 %collective-permute-done.10.refs_2_ = bf16[5,144,128]{2,1,0:T(8,128)(2,1)S(1)} collective-permute-done((bf16[5,144,128]{2,1,0:T(8,128)(2,1)S(1)}, bf16[5,144,128]{2,1,0:T(8,128)(2,1)S(1)}, u32[]{:S(2)}, u32[]{:S(2)}) %collective-permute-start.10) | collective-permute-done | bytes 184352 | tf_op jit(solution)/shard_map/ppermute | solution.py:714
  110.4 10.4 %collective-permute-done.13.refs_2_ = bf16[5,144,128]{2,1,0:T(8,128)(2,1)S(1)} collective-permute-done((bf16[5,144,128]{2,1,0:T(8,128)(2,1)S(1)}, bf16[5,144,128]{2,1,0:T(8,128)(2,1)S(1)}, u32[]{:S(2)}, u32[]{:S(2)}) %collective-permute-start.13) | collective-permute-done | bytes 184352 | tf_op jit(solution)/shard_map/ppermute | solution.py:714
  120.8 7.1 %query_gradient.1 = (bf16[256,1024]{1,0:T(8,128)(2,1)S(1)}, bf16[256,1024]{1,0:T(8,128)(2,1)S(1)}, f32[4,128]{1,0:T(4,128)}) custom-call(s32[33]{0:T(128)S(1)} %pad_add_fusion.tab_ref, s32[4,128]{1,0:T(4,128)S(1)} %bitcast.35, bf16[512,1024]{1,0:T(8,128)(2,1)} %copy-done.25, bf16[5,144,128]{2,1,0:T(8,128)(2,1)S(1)} %powers.1.refs_0_, ...), custom_call_target="tpu_custom_call" | custom-call | flops 6600000000 | tf_op jit(solution)/shard_map/query_gradient/pallas_call | solution.py:312
  132.9 7.4 %passage_terms.1 = (bf16[4,128,1024]{2,1,0:T(8,128)(2,1)}, bf16[2,2,128,1024]{3,2,1,0:T(8,128)(2,1)}, bf16[2,2,128,1024]{3,2,1,0:T(8,128)(2,1)}, bf16[2,2,128,10...) custom-call(s32[33]{0:T(128)S(1)} %pad_add_fusion.tab_ref, s32[4,128]{1,0:T(4,128)S(1)} %bitcast.36, ...), custom_call_target="tpu_custom_call" | custom-call | flops 6600000000 | tf_op jit(solution)/shard_map/passage_terms/pallas_call | solution.py:312
  148.1 6.2 %collective-permute-done.21.refs_1_ = bf16[256,1024]{1,0:T(8,128)(2,1)S(1)} collective-permute-done((bf16[256,1024]{1,0:T(8,128)(2,1)S(1)}, bf16[256,1024]{1,0:T(8,128)(2,1)S(1)}, u32[]{:S(2)}, u32[]{:S(2)}) %collective-permute-start.21) | collective-permute-done | bytes 524320 | tf_op jit(solution)/shard_map/ppermute | solution.py:635
  157.0 5.9 %collective-permute-start.23 = (bf16[256,1024]{1,0:T(8,128)(2,1)}, bf16[256,1024]{1,0:T(8,128)(2,1)}, u32[]{:S(2)}, u32[]{:S(2)}) collective-permute-start(bf16[256,1024]{1,0:T(8,128)(2,1)} %get-tuple-element.50), channel_id=1, source_target_pairs={{0,1},{1,0},{2,3},{3,2},{4,5},{5,4},{6,7},{7,6},{8,9},{9,8},{10,11... | collective-permute-start | bytes 1572872 | tf_op jit(solution)/shard_map/ppermute | solution.py:635
  166.4 6.0 %collective-permute-done.23.refs_1_.refs_2_ = bf16[256,1024]{1,0:T(8,128)(2,1)} collective-permute-done((bf16[256,1024]{1,0:T(8,128)(2,1)}, bf16[256,1024]{1,0:T(8,128)(2,1)}, u32[]{:S(2)}, u32[]{:S(2)}) %collective-permute-start.23) | collective-permute-done | bytes 524320 | tf_op jit(solution)/shard_map/ppermute | solution.py:635
  180.5 3.7 %weight_slabs.5.refs_7_.earlier_ref = bf16[4,512,1024]{2,1,0:T(8,128)(2,1)S(1)} custom-call(s32[4]{0:T(128)S(1)} %pad_add_fusion.2.tab_ref, bf16[512,4096]{1,0:T(8,128)(2,1)S(1)} %copy-done.8, bf16[256,1024]{1,0:T(8,128)(2,1)S(1)} %copy-done.10, bf16[256,1024]{1,0:T(8,128)(2,1)S(1)} %get-tuple-element.47.bottom_ref), custom_call_target="tpu_custom_call" | custom-call | flops 1100000000 | tf_op jit(solution)/shard_map/weight_slabs/pallas_call | solution.py:428
  186.2 3.7 %weight_slabs.4.refs_6_.refs_0_ = bf16[4,512,1024]{2,1,0:T(8,128)(2,1)S(1)} custom-call(s32[4]{0:T(128)S(1)} %pad_add_fusion.4.tab_ref, bf16[512,4096]{1,0:T(8,128)(2,1)S(1)} %copy-done.8, bf16[256,1024]{1,0:T(8,128)(2,1)S(1)} %copy-done.10, bf16[256,1024]{1,0:T(8,128)(2,1)S(1)} %get-tuple-element.47.bottom_ref), custom_call_target="tpu_custom_call" | custom-call | flops 1100000000 | tf_op jit(solution)/shard_map/weight_slabs/pallas_call | solution.py:428
  199.7 4.1 %slab_product.2.refs_9_.bottom_ref = bf16[256,1024]{1,0:T(8,128)(2,1)S(1)} custom-call(s32[1]{0:T(128)} %bitcast.tab_ref, f32[256,1024]{1,0:T(8,128)S(1)} %copy-done.28, bf16[256,1024]{1,0:T(8,128)(2,1)} %collective-permute-done.18.refs_0_, bf16[256,1024]{1,0:T(8,128)(2,1)S(1)} %copy-done.37, bf16[256,1024]{1,0:T(8,128)(2,1)} %collective-permute-done.23.refs_1_.refs_2_, ...), custom_call_target="tpu_custom_call" | custom-call | flops 1100000000 | tf_op jit(solution)/shard_map/slab_product/pallas_call | solution.py:543
  203.9 5.0 %collective-permute-done.16.refs_2_.refs_4_ = bf16[2,2,128,1024]{3,2,1,0:T(8,128)(2,1)} collective-permute-done((bf16[2,2,128,1024]{3,2,1,0:T(8,128)(2,1)}, bf16[2,2,128,1024]{3,2,1,0:T(8,128)(2,1)}, u32[]{:S(2)}, u32[]{:S(2)}) %collective-permute-start.16) | collective-permute-done | bytes 1048608 | tf_op jit(solution)/shard_map/ppermute | solution.py:713
  210.4 4.1 %collective-permute-done.26.refs_1_.refs_3_.refs_5_.refs_7_ = bf16[4,2,128,1024]{3,2,1,0:T(8,128)(2,1)S(1)} collective-permute-done((bf16[4,2,128,1024]{3,2,1,0:T(8,128)(2,1)S(1)}, bf16[4,2,128,1024]{3,2,1,0:T(8,128)(2,1)S(1)}, u32[]{:S(2)}, u32[]{:S(2)}) %collective-permute-start.26) | collective-permute-done | bytes 2097184 | tf_op jit(solution)/shard_map/ppermute | solution.py:713
  219.0 3.7 %weight_slabs.6.refs_2_ = bf16[4,512,1024]{2,1,0:T(8,128)(2,1)S(1)} custom-call(s32[4]{0:T(128)S(1)} %pad_add_fusion.4.tab_ref, bf16[512,4096]{1,0:T(8,128)(2,1)S(1)} %copy-done.43, bf16[256,1024]{1,0:T(8,128)(2,1)S(1)} %get-tuple-element.54.top_ref, bf16[256,1024]{1,0:T(8,128)(2,1)S(1)} %get-tuple-element.55.bottom_ref, ...), custom_call_target="tpu_custom_call" | custom-call | flops 4400000000 | tf_op jit(solution)/shard_map/weight_slabs/pallas_call | solution.py:428
  228.1 11.5 %collective-permute-start.35 = (bf16[256,1024]{1,0:T(8,128)(2,1)S(1)}, bf16[256,1024]{1,0:T(8,128)(2,1)S(1)}, u32[]{:S(2)}, u32[]{:S(2)}) collective-permute-start(bf16[256,1024]{1,0:T(8,128)(2,1)S(1)} %pass_on.9.refs_0_), channel_id=1, source_target_pairs={{0,1},{1,0},{2,3},{3,2},{4,5},{5,4},{6,7},{7,6},{8,9},{9,8},{10,11... | collective-permute-start | bytes 1572872 | tf_op jit(solution)/shard_map/ppermute | solution.py:635
  240.3 4.2 %weight_slabs.7 = (bf16[2,512,512]{2,1,0:T(8,128)(2,1)S(1)}, bf16[2,512,512]{2,1,0:T(8,128)(2,1)S(1)}, bf16[2,512,512]{2,1,0:T(8,128)(2,1)S(1)}, bf16[2,512,512]{2,1,0:T(8,128)(2,1)S(1)}) custom-call(s32[4]{0:T(128)S(1)} %pad_add_fusion.2.tab_ref, bf16[512,4096]{1,0:T(8,128)(2,1)S(1)} %copy-done.43, bf16[256,1024]{1,0:T(8,128)(2,1)S(1)} %get-tuple-element.54.top_ref, ...), custom_call_target="tpu_custom_call" | custom-call | flops 5500000256 | tf_op jit(solution)/shard_map/weight_slabs/pallas_call | solution.py:428
  252.4 6.3 %collective-permute-start.37 = (bf16[256,1024]{1,0:T(8,128)(2,1)S(1)}, bf16[256,1024]{1,0:T(8,128)(2,1)S(1)}, u32[]{:S(2)}, u32[]{:S(2)}) collective-permute-start(bf16[256,1024]{1,0:T(8,128)(2,1)S(1)} %get-tuple-element.64), channel_id=1, source_target_pairs={{0,1},{1,0},{2,3},{3,2},{4,5},{5,4},{6,7},{7,6},{8,9},{9,8},{10,11... | collective-permute-start | bytes 1572872 | tf_op jit(solution)/shard_map/ppermute | solution.py:635
  258.8 10.1 %collective-permute-done.37.refs_1_.refs_2_ = bf16[256,1024]{1,0:T(8,128)(2,1)S(1)} collective-permute-done((bf16[256,1024]{1,0:T(8,128)(2,1)S(1)}, bf16[256,1024]{1,0:T(8,128)(2,1)S(1)}, u32[]{:S(2)}, u32[]{:S(2)}) %collective-permute-start.37) | collective-permute-done | bytes 524320 | tf_op jit(solution)/shard_map/ppermute | solution.py:635
  (246 shorter events, 127.8 us)
Async XLA Ops:
  13.9 18.2 %collective-permute-start.3 = (bf16[512,512]{1,0:T(8,128)(2,1)}, bf16[512,512]{1,0:T(8,128)(2,1)S(1)}, u32[]{:S(2)}, u32[]{:S(2)}) collective-permute-start(bf16[512,512]{1,0:T(8,128)(2,1)} %fusion.4.refs_0_.refs_4_.refs_6_), channel_id=1, source_target_pairs={{0,16},{4,20},{8,24},{12,28},{16,0},{20,4},{24,8},{28,12},{1,17},{... | collective-permute-start | bytes 1572872 | tf_op jit(solution)/shard_map/ppermute | solution.py:713
  16.9 15.2 %collective-permute-start.1 = (bf16[512,512]{1,0:T(8,128)(2,1)}, bf16[512,512]{1,0:T(8,128)(2,1)S(1)}, u32[]{:S(2)}, u32[]{:S(2)}) collective-permute-start(bf16[512,512]{1,0:T(8,128)(2,1)} %fusion.4.refs_0_.refs_4_.refs_6_), channel_id=1, source_target_pairs={{0,8},{4,12},{8,0},{12,4},{16,24},{20,28},{24,16},{28,20},{1,9},{5... | collective-permute-start | bytes 1572872 | tf_op jit(solution)/shard_map/ppermute | solution.py:713
  21.5 18.7 %collective-permute-start.4 = (bf16[512,512]{1,0:T(8,128)(2,1)}, bf16[512,512]{1,0:T(8,128)(2,1)S(1)}, u32[]{:S(2)}, u32[]{:S(2)}) collective-permute-start(bf16[512,512]{1,0:T(8,128)(2,1)} %fusion.7.refs_1_.refs_5_.refs_7_), channel_id=1, source_target_pairs={{0,16},{4,20},{8,24},{12,28},{16,0},{20,4},{24,8},{28,12},{1,17},{... | collective-permute-start | bytes 1572872 | tf_op jit(solution)/shard_map/ppermute | solution.py:713
  22.0 19.7 %collective-permute-start.2 = (bf16[512,512]{1,0:T(8,128)(2,1)}, bf16[512,512]{1,0:T(8,128)(2,1)S(1)}, u32[]{:S(2)}, u32[]{:S(2)}) collective-permute-start(bf16[512,512]{1,0:T(8,128)(2,1)} %fusion.7.refs_1_.refs_5_.refs_7_), channel_id=1, source_target_pairs={{0,8},{4,12},{8,0},{12,4},{16,24},{20,28},{24,16},{28,20},{1,9},{5... | collective-permute-start | bytes 1572872 | tf_op jit(solution)/shard_map/ppermute | solution.py:713
  24.3 56.5 %all-to-all-start.1 = ((bf16[4,128,1024]{2,1,0:T(8,128)(2,1)}), bf16[4,128,1024]{2,1,0:T(8,128)(2,1)}, u32[]{:S(2)}, u32[]{:S(2)}) async-start(bf16[4,128,1024]{2,1,0:T(8,128)(2,1)} %dynamic-slice_bitcast_fusion), calls=%async_computation.1 | async-start | bytes 2097152 | tf_op jit(solution)/shard_map/all_to_all | solution.py:718
  29.7 162.3 %all-gather.2.cloned.1.call-start = ((), (), s32[]{:S(2)}) async-start(), calls=%async_computation.2 | async-start | bytes 9437184 | tf_op jit(solution)/shard_map/all_gather | solution.py:745
  32.1 31.7 %collective-permute-start = (bf16[2,512,512]{2,1,0:T(8,128)(2,1)}, bf16[2,512,512]{2,1,0:T(8,128)(2,1)S(1)}, u32[]{:S(2)}, u32[]{:S(2)}) collective-permute-start(bf16[2,512,512]{2,1,0:T(8,128)(2,1)} %stack.85), channel_id=1, source_target_pairs={{0,4},{4,0},{8,12},{12,8},{16,20},{20,16},{24,28},{28,24},{1,5},{5... | collective-permute-start | bytes 3145736 | tf_op jit(solution)/shard_map/ppermute | solution.py:713
  46.4 19.9 %collective-permute-start.5 = (bf16[4,512,512]{2,1,0:T(8,128)(2,1)}, bf16[4,512,512]{2,1,0:T(8,128)(2,1)S(1)}, u32[]{:S(2)}, u32[]{:S(2)}) collective-permute-start(bf16[4,512,512]{2,1,0:T(8,128)(2,1)} %stack.86), channel_id=1, source_target_pairs={{0,4},{4,0},{8,12},{12,8},{16,20},{20,16},{24,28},{28,24},{1,5},{5... | collective-permute-start | bytes 6291464 | tf_op jit(solution)/shard_map/ppermute | solution.py:713
  46.4 14.5 %collective-permute-start.6 = (bf16[512,512]{1,0:T(8,128)(2,1)}, bf16[512,512]{1,0:T(8,128)(2,1)S(1)}, u32[]{:S(2)}, u32[]{:S(2)}) collective-permute-start(bf16[512,512]{1,0:T(8,128)(2,1)} %copy-done.16), channel_id=1, source_target_pairs={{0,16},{4,20},{8,24},{12,28},{16,0},{20,4},{24,8},{28,12},{1,17},{... | collective-permute-start | bytes 1572872 | tf_op jit(solution)/shard_map/ppermute | solution.py:713
  46.7 14.3 %collective-permute-start.7 = (bf16[512,512]{1,0:T(8,128)(2,1)}, bf16[512,512]{1,0:T(8,128)(2,1)S(1)}, u32[]{:S(2)}, u32[]{:S(2)}) collective-permute-start(bf16[512,512]{1,0:T(8,128)(2,1)} %copy-done.19), channel_id=1, source_target_pairs={{0,8},{4,12},{8,0},{12,4},{16,24},{20,28},{24,16},{28,20},{1,9},{5... | collective-permute-start | bytes 1572872 | tf_op jit(solution)/shard_map/ppermute | solution.py:713
  85.2 16.3 %collective-permute-start.10 = (bf16[5,144,128]{2,1,0:T(8,128)(2,1)S(1)}, bf16[5,144,128]{2,1,0:T(8,128)(2,1)S(1)}, u32[]{:S(2)}, u32[]{:S(2)}) collective-permute-start(bf16[5,144,128]{2,1,0:T(8,128)(2,1)S(1)} %copy-done.45), channel_id=1, source_target_pairs={{0,2},{1,3},{2,0},{3,1},{4,6},{5,7},{6,4},{7,5},{8,10},{9,11},{10,... | collective-permute-start | bytes 552968 | tf_op jit(solution)/shard_map/ppermute | solution.py:714
  104.9 15.9 %collective-permute-start.13 = (bf16[5,144,128]{2,1,0:T(8,128)(2,1)S(1)}, bf16[5,144,128]{2,1,0:T(8,128)(2,1)S(1)}, u32[]{:S(2)}, u32[]{:S(2)}) collective-permute-start(bf16[5,144,128]{2,1,0:T(8,128)(2,1)S(1)} %powers.1.refs_0_), channel_id=1, source_target_pairs={{0,2},{1,3},{2,0},{3,1},{4,6},{5,7},{6,4},{7,5},{8,10},{9,11},{10,... | collective-permute-start | bytes 552968 | tf_op jit(solution)/shard_map/ppermute | solution.py:714
  157.0 15.4 %collective-permute-start.23 = (bf16[256,1024]{1,0:T(8,128)(2,1)}, bf16[256,1024]{1,0:T(8,128)(2,1)}, u32[]{:S(2)}, u32[]{:S(2)}) collective-permute-start(bf16[256,1024]{1,0:T(8,128)(2,1)} %get-tuple-element.50), channel_id=1, source_target_pairs={{0,1},{1,0},{2,3},{3,2},{4,5},{5,4},{6,7},{7,6},{8,9},{9,8},{10,11... | collective-permute-start | bytes 1572872 | tf_op jit(solution)/shard_map/ppermute | solution.py:635
  162.9 41.0 %collective-permute-start.15 = (bf16[2,2,128,1024]{3,2,1,0:T(8,128)(2,1)}, bf16[2,2,128,1024]{3,2,1,0:T(8,128)(2,1)S(1)}, u32[]{:S(2)}, u32[]{:S(2)}) collective-permute-start(bf16[2,2,128,1024]{3,2,1,0:T(8,128)(2,1)} %get-tuple-element.44), channel_id=1, source_target_pairs={{0,8},{4,12},{8,0},{12,4},{16,24},{20,28},{24,16},{28,20},{1,9},{5... | collective-permute-start | bytes 3145736 | tf_op jit(solution)/shard_map/ppermute | solution.py:713
  164.4 44.5 %collective-permute-start.16 = (bf16[2,2,128,1024]{3,2,1,0:T(8,128)(2,1)}, bf16[2,2,128,1024]{3,2,1,0:T(8,128)(2,1)}, u32[]{:S(2)}, u32[]{:S(2)}) collective-permute-start(bf16[2,2,128,1024]{3,2,1,0:T(8,128)(2,1)} %get-tuple-element.45), channel_id=1, source_target_pairs={{0,16},{4,20},{8,24},{12,28},{16,0},{20,4},{24,8},{28,12},{1,17},{... | collective-permute-start | bytes 3145736 | tf_op jit(solution)/shard_map/ppermute | solution.py:713
  165.9 43.0 %collective-permute-start.17 = (bf16[2,2,128,1024]{3,2,1,0:T(8,128)(2,1)}, bf16[2,2,128,1024]{3,2,1,0:T(8,128)(2,1)}, u32[]{:S(2)}, u32[]{:S(2)}) collective-permute-start(bf16[2,2,128,1024]{3,2,1,0:T(8,128)(2,1)} %get-tuple-element.46), channel_id=1, source_target_pairs={{0,24},{4,28},{8,16},{12,20},{16,8},{20,12},{24,0},{28,4},{1,25},{... | collective-permute-start | bytes 3145736 | tf_op jit(solution)/shard_map/ppermute | solution.py:713
  177.2 31.7 %collective-permute-start.24 = (bf16[256,1024]{1,0:T(8,128)(2,1)}, bf16[256,1024]{1,0:T(8,128)(2,1)}, u32[]{:S(2)}, u32[]{:S(2)}) collective-permute-start(bf16[256,1024]{1,0:T(8,128)(2,1)} %get-tuple-element.51), channel_id=1, source_target_pairs={{0,1},{1,0},{2,3},{3,2},{4,5},{5,4},{6,7},{7,6},{8,9},{9,8},{10,11... | collective-permute-start | bytes 1572872 | tf_op jit(solution)/shard_map/ppermute | solution.py:635
  178.9 30.0 %collective-permute-start.25 = (bf16[256,1024]{1,0:T(8,128)(2,1)}, bf16[256,1024]{1,0:T(8,128)(2,1)}, u32[]{:S(2)}, u32[]{:S(2)}) collective-permute-start(bf16[256,1024]{1,0:T(8,128)(2,1)} %get-tuple-element.52), channel_id=1, source_target_pairs={{1,2},{2,1},{5,6},{6,5},{9,10},{10,9},{13,14},{14,13},{17,18},{18,... | collective-permute-start | bytes 1572872 | tf_op jit(solution)/shard_map/ppermute | solution.py:636
  222.7 17.5 %collective-permute-start.27 = (bf16[4,512,1024]{2,1,0:T(8,128)(2,1)S(1)}, bf16[4,512,1024]{2,1,0:T(8,128)(2,1)S(1)}, u32[]{:S(2)}, u32[]{:S(2)}) collective-permute-start(bf16[4,512,1024]{2,1,0:T(8,128)(2,1)S(1)} %weight_slabs.6.refs_2_), channel_id=1, source_target_pairs={{0,4},{4,0},{8,12},{12,8},{16,20},{20,16},{24,28},{28,24},{1,5},{5... | collective-permute-start | bytes 12582920 | tf_op jit(solution)/shard_map/ppermute | solution.py:713
  223.6 15.9 %collective-permute-start.33 = (bf16[256,1024]{1,0:T(8,128)(2,1)S(1)}, bf16[256,1024]{1,0:T(8,128)(2,1)S(1)}, u32[]{:S(2)}, u32[]{:S(2)}) collective-permute-start(bf16[256,1024]{1,0:T(8,128)(2,1)S(1)} %get-tuple-element.55.bottom_ref), channel_id=1, source_target_pairs={{0,1},{1,0},{2,3},{3,2},{4,5},{5,4},{6,7},{7,6},{8,9},{9,8},{10,11... | collective-permute-start | bytes 1572872 | tf_op jit(solution)/shard_map/ppermute | solution.py:630
  228.1 23.1 %collective-permute-start.35 = (bf16[256,1024]{1,0:T(8,128)(2,1)S(1)}, bf16[256,1024]{1,0:T(8,128)(2,1)S(1)}, u32[]{:S(2)}, u32[]{:S(2)}) collective-permute-start(bf16[256,1024]{1,0:T(8,128)(2,1)S(1)} %pass_on.9.refs_0_), channel_id=1, source_target_pairs={{0,1},{1,0},{2,3},{3,2},{4,5},{5,4},{6,7},{7,6},{8,9},{9,8},{10,11... | collective-permute-start | bytes 1572872 | tf_op jit(solution)/shard_map/ppermute | solution.py:635
  244.5 27.1 %collective-permute-start.28 = (bf16[2,512,512]{2,1,0:T(8,128)(2,1)S(1)}, bf16[2,512,512]{2,1,0:T(8,128)(2,1)S(1)}, u32[]{:S(2)}, u32[]{:S(2)}) collective-permute-start(bf16[2,512,512]{2,1,0:T(8,128)(2,1)S(1)} %get-tuple-element.57), channel_id=1, source_target_pairs={{0,8},{4,12},{8,0},{12,4},{16,24},{20,28},{24,16},{28,20},{1,9},{5... | collective-permute-start | bytes 3145736 | tf_op jit(solution)/shard_map/ppermute | solution.py:713
  245.6 26.0 %collective-permute-start.29 = (bf16[2,512,512]{2,1,0:T(8,128)(2,1)S(1)}, bf16[2,512,512]{2,1,0:T(8,128)(2,1)S(1)}, u32[]{:S(2)}, u32[]{:S(2)}) collective-permute-start(bf16[2,512,512]{2,1,0:T(8,128)(2,1)S(1)} %get-tuple-element.59), channel_id=1, source_target_pairs={{0,16},{4,20},{8,24},{12,28},{16,0},{20,4},{24,8},{28,12},{1,17},{... | collective-permute-start | bytes 3145736 | tf_op jit(solution)/shard_map/ppermute | solution.py:713
  252.4 16.5 %collective-permute-start.37 = (bf16[256,1024]{1,0:T(8,128)(2,1)S(1)}, bf16[256,1024]{1,0:T(8,128)(2,1)S(1)}, u32[]{:S(2)}, u32[]{:S(2)}) collective-permute-start(bf16[256,1024]{1,0:T(8,128)(2,1)S(1)} %get-tuple-element.64), channel_id=1, source_target_pairs={{0,1},{1,0},{2,3},{3,2},{4,5},{5,4},{6,7},{7,6},{8,9},{9,8},{10,11... | collective-permute-start | bytes 1572872 | tf_op jit(solution)/shard_map/ppermute | solution.py:635
  (82 other events, 703.7 us)
Sparse Core Ops, SparseCore 0:
  83.4 55.6 all-gather.1
